TPU v7x, 128 devices: a whole 4x4x4 slice. The times are simulated.
128 devices in a mesh: group: 8 (over x_lo, z), member: 16 (over y, x_hi, core).
Axes of the slice: x: 4 (x_hi: 2, x_lo: 2; x = x_hi * 2 + x_lo), y: 4, z: 4, core: 2. Of those that a mesh axis runs over, the one named last changes fastest.
Arguments:
- entities: float32 [8, 4096, 400], P('group', 'member'), may hold values from -4 to 4
- ent_state: float32 [8, 4096], P('group', 'member'), may hold values from 0.05 to 0.5
- relations: float32 [4096, 400], replicated, may hold values from -6 to 6
- rel_state: float32 [4096], replicated, may hold values from 0.05 to 0.5
- lhs_rows: int32 [8, 65536], P('group', 'member'), may hold values from 0 to 255
- rhs_owner: int32 [8, 65536, 1], P('group', 'member'), may hold values from 0 to 15; in each aligned block of 4096 rows (0 to 4095, 4096 to 8191, ..., all dimensions but the last counted through in order) at most 320 rows name the same one
- rhs_off: int32 [8, 65536], P('group', 'member'), may hold values from 0 to 255
- neg_owner: int32 [8, 64000, 1], P('group', 'member'), may hold values from 0 to 15; in each aligned block of 4000 rows (0 to 3999, 4000 to 7999, ..., all dimensions but the last counted through in order) at most 312 rows name the same one
- neg_off: int32 [8, 64000], P('group', 'member'), may hold values from 0 to 255
- rel_ids: int32 [8, 65536], P('group', 'member'), may hold values from 0 to 4095
- counts: int32 [8, 16], P('group', 'member'), may hold values from 1024 to 4096, as said below
Outputs:
- new_entities: float32 [8, 4096, 400], P('group', 'member')
- new_ent_state: float32 [8, 4096], P('group', 'member')
- new_relations: float32 [4096, 400], replicated
- new_rel_state: float32 [4096], replicated
Inputs may be any that keep to these rules, and one draw needn't show every extreme that they name: `rhs_owner`: among the 4096 slots of one device at most 320 name one block, and some block is named by exactly 320. `neg_owner`: among the 4000 negatives of one device at most 312 name one block, and some block is named by exactly 312. `counts`: some device is full in every draw.
All inputs are finite; a program needn't handle non-finite values.
Results may differ from a plain program's by a relative error of at most 0.0001.
Values sent between devices are 32-bit elements; how exact they have to be, the bound alone decides.
A program may use at most 256 MiB of HBM per device.

v0:
```python
import jax
import jax.numpy as jnp
from jax import lax
from jax.sharding import PartitionSpec as P

SPAN = 512
NEG = 500


STEP_SIZE = 0.1


def from_behind(array, axis, by):
    devices = lax.axis_size(axis)
    return lax.ppermute(array, axis, [(i, (i + by) % devices) for i in range(devices)])


def on_device(
    entities,
    ent_state,
    relations,
    rel_state,
    lhs_rows,
    rhs_owner,
    rhs_off,
    neg_owner,
    neg_off,
    rel_ids,
    counts,
):
    shard = entities[0]
    rows = shard.shape[0]
    width = shard.shape[1]
    right = from_behind(shard, "group", -1)
    lhs = lhs_rows[0]
    rown = rhs_owner[0, :, 0]
    roff = rhs_off[0]
    nown = neg_owner[0, :, 0]
    noff = neg_off[0]
    rid = rel_ids[0]
    edges = lhs.shape[0]
    live = (jnp.arange(edges, dtype=jnp.int32) < counts[0, 0]).astype(jnp.float32)
    left_vec = shard[lhs]
    rel_vec = relations[rid]
    query = left_vec * rel_vec
    slab = lax.all_gather(right, "member", axis=0, tiled=True)
    ridx = rown * rows + roff
    nidx = nown * rows + noff
    right_vec = slab[ridx]
    neg_flat = slab[nidx]
    pos = jnp.sum(query * right_vec, axis=1)
    nchunk = edges // SPAN
    query_c = query.reshape(nchunk, SPAN, width)
    neg_vec = neg_flat.reshape(nchunk, NEG, width)
    neg = jnp.einsum("cjd,cnd->cjn", query_c, neg_vec, precision=lax.Precision.HIGHEST)
    dpos = -jax.nn.sigmoid(-pos) * live
    dneg = jax.nn.sigmoid(neg) * live.reshape(nchunk, SPAN, 1) / NEG
    grad_query = dpos[:, None] * right_vec + jnp.einsum(
        "cjn,cnd->cjd", dneg, neg_vec, precision=lax.Precision.HIGHEST
    ).reshape(edges, width)
    grad_right = dpos[:, None] * query
    grad_neg = jnp.einsum("cjn,cjd->cnd", dneg, query_c, precision=lax.Precision.HIGHEST).reshape(
        nchunk * NEG, width
    )
    left_grad = jnp.zeros((rows, width), jnp.float32).at[lhs].add(grad_query * rel_vec)
    start = jnp.int32(0)
    count = rows * lax.axis_size("member")
    inside_r = (ridx >= start) & (ridx < start + count)
    inside_n = (nidx >= start) & (nidx < start + count)
    local_r = jnp.where(inside_r, ridx, count)
    local_n = jnp.where(inside_n, nidx, count)
    term = jnp.zeros((count, width), jnp.float32)
    term = term.at[local_r].add(grad_right, mode="drop")
    right_grad = lax.psum_scatter(
        term.at[local_n].add(grad_neg, mode="drop"), "member", scatter_dimension=0, tiled=True
    )
    returned = from_behind(right_grad, "group", 1)
    grad_total = left_grad + returned
    new_state = ent_state[0] + jnp.mean(grad_total * grad_total, axis=1)
    new_shard = shard - STEP_SIZE * grad_total / jnp.sqrt(new_state)[:, None]
    rel_grad = jnp.zeros(relations.shape, jnp.float32).at[rid].add(grad_query * left_vec)
    rel_total = lax.psum(rel_grad, ("group", "member"))
    rel_new_state = rel_state + jnp.mean(rel_total * rel_total, axis=1)
    rel_new = relations - STEP_SIZE * rel_total / jnp.sqrt(rel_new_state)[:, None]
    return (new_shard[None], new_state[None], rel_new, rel_new_state)


def solution(mesh):
    in_specs = (
        P("group", "member", None),
        P("group", "member"),
        P(),
        P(),
        P("group", "member"),
        P("group", "member", None),
        P("group", "member"),
        P("group", "member", None),
        P("group", "member"),
        P("group", "member"),
        P("group", "member"),
    )
    out_specs = (P("group", "member", None), P("group", "member"), P(), P())
    return jax.shard_map(
        on_device, mesh=mesh, in_specs=in_specs, out_specs=out_specs, check_vma=False
    )
```

profile of v0, /device:TPU:1, one launch (start us, length us, event | category | flops | bytes accessed | tf_op | source)
XLA Modules:
  0.0 568.1 jit_solution(3129964892990514801)
XLA Ops:
  8.4 5.6 collective-permute-start
  14.0 10.6 %collective-permute-done = f32[256,400]{1,0:T(8,128)S(1)} collective-permute-done((f32[256,400]{1,0:T(8,128)S(1)}, f32[256,400]{1,0:T(8,128)S(1)}, u32[]{:S(2)}, u32[]{:S(2)}) %collective-permute-start) | collective-permute-done | bytes 409632 | tf_op jit(solution)/shard_map/ppermute | solution.py:15
  27.5 16.8 %gather_fusion = f32[4096,400]{1,0:T(8,128)} fusion(f32[256,400]{1,0:T(8,128)S(1)} %bitcast.53, s32[4096]{0:T(1024)S(1)} %broadcast_clamp_fusion.2), kind=kCustom, calls=%fused_computation | custom fusion | bytes 13123584 | tf_op jit(solution)/shard_map/gather | solution.py:43
  44.2 8.5 %copy.25 = f32[4096,400]{1,0:T(8,128)} copy(f32[4096,400]{0,1:T(8,128)} %param.13) | data formatting | bytes 13107200 | tf_op args[2]
  52.9 21.4 %gather_fusion.1 = f32[4096,400]{1,0:T(8,128)} fusion(f32[4096,400]{1,0:T(8,128)} %copy.25, s32[4096]{0:T(1024)S(1)} %broadcast_clamp_fusion.1), kind=kCustom, calls=%fused_computation.1 | custom fusion | bytes 13123584 | tf_op jit(solution)/shard_map/gather | solution.py:44
  74.5 27.3 %all-gather.2.cloned.1.call-done = f32[4096,400]{1,0:T(8,128)} async-done(((f32[256,400]{1,0:T(8,128)}), f32[4096,400]{1,0:T(8,128)}) %all-gather.2.cloned.1.call-update) | async-done | bytes 6553616 | tf_op jit(solution)/shard_map/all_gather | solution.py:46
  101.7 21.2 %gather_fusion.3 = f32[4000,400]{1,0:T(8,128)} fusion(f32[4096,400]{1,0:T(8,128)} %all-gather.2.cloned.1.call-done, s32[4096]{0:T(1024)S(1)} %pad_clamp_fusion), kind=kCustom, calls=%fused_computation.3 | custom fusion | bytes 12816000 | tf_op jit(solution)/shard_map/gather | solution.py:50
  123.0 7.1 %reshape.305 = f32[8,500,400]{2,1,0:T(8,128)} reshape(f32[4000,400]{1,0:T(8,128)} %gather_fusion.3) | data formatting | bytes 12800000 | tf_op jit(solution)/shard_map/reshape | solution.py:54
  130.1 21.3 %gather_fusion.2 = f32[4096,400]{1,0:T(8,128)} fusion(f32[4096,400]{1,0:T(8,128)} %all-gather.2.cloned.1.call-done, s32[4096]{0:T(1024)S(1)} %broadcast_clamp_fusion), kind=kCustom, calls=%fused_computation.2 | custom fusion | bytes 13123584 | tf_op jit(solution)/shard_map/gather | solution.py:49
  151.4 9.0 %multiply_reduce_fusion.1 = (f32[4096]{0:T(1024)S(1)}, f32[4096,400]{1,0:T(8,128)S(1)}) fusion(f32[4096,400]{1,0:T(8,128)} %gather_fusion.2, f32[4096,400]{1,0:T(8,128)} %gather_fusion, f32[4096,400]{1,0:T(8,128)} %gather_fusion.1), kind=kLoop, calls=%fused_computation.17 | loop fusion | flops 4911104 | bytes 26230784 | tf_op jit(solution)/shard_map/reduce_sum | solution.py:51
  160.5 32.6 %multiply_multiply_fusion = f32[8,512,500]{1,2,0:T(8,128)} fusion(f32[8,512]{1,0:T(8,128)S(1)} %fusion.9, f32[8,512,400]{2,1,0:T(8,128)S(1)} %bitcast.54, f32[8,500,400]{2,1,0:T(8,128)} %reshape.305), kind=kOutput, calls=%fused_computation.18 | convolution fusion | flops 9840640000 | bytes 21161984 | tf_op jit(solution)/shard_map/cjd,cnd->cjn/dot_general | solution.py:55
  193.0 19.9 %fusion.12 = f32[8,512,400]{2,1,0:T(8,128)} fusion(f32[8,512,500]{1,2,0:T(8,128)} %multiply_multiply_fusion, f32[8,500,400]{2,1,0:T(8,128)} %reshape.305), kind=kOutput, calls=%fused_computation.47 | convolution fusion | flops 9830400000 | bytes 21145600 | tf_op jit(solution)/shard_map/reshape | solution.py:60
  212.9 6.2 %bitcast_add_fusion = f32[4096,400]{1,0:T(8,128)} fusion(f32[8,512,400]{2,1,0:T(8,128)} %fusion.12, f32[4096,400]{1,0:T(8,128)S(1)} %bitcast.57, f32[4096]{0:T(1024)S(1)} %negate_select_fusion), kind=kLoop, calls=%fused_computation.8 | loop fusion | flops 3276800 | bytes 19677184 | tf_op jit(solution)/shard_map/add | solution.py:58
  219.1 30.1 %scatter_custom_fusion.3 = f32[4096,400]{1,0:T(8,128)} fusion(s32[4096]{0:T(1024)S(1)} %bitcast.62, f32[4096,400]{1,0:T(8,128)} %bitcast_add_fusion, f32[4096,400]{1,0:T(8,128)} %gather_fusion, f32[]{:T(128)} %constant.9.clone.1), kind=kCustom, calls=%fused_computation.11 | custom fusion | flops 3276800 | bytes 19660804 | tf_op jit(solution)/shard_map/scatter-add | solution.py:81
  249.2 19.4 %fusion.11 = f32[8,500,400]{2,1,0:T(8,128)} fusion(f32[8,512,500]{1,2,0:T(8,128)} %multiply_multiply_fusion, f32[8,512,400]{2,1,0:T(8,128)} %bitcast.55), kind=kOutput, calls=%fused_computation.46 | convolution fusion | flops 9830400000 | bytes 21145600 | tf_op jit(solution)/shard_map/reshape | solution.py:62
  268.7 7.3 %reshape.304 = f32[4000,400]{1,0:T(8,128)} reshape(f32[8,500,400]{2,1,0:T(8,128)} %fusion.11) | data formatting | bytes 12800000 | tf_op jit(solution)/shard_map/reshape | solution.py:62
  275.9 31.1 %scatter_custom_fusion = f32[4096,400]{1,0:T(8,128)} fusion(s32[4096]{0:T(1024)S(1)} %bitcast.65, f32[4096,400]{1,0:T(8,128)} %copy-done.2, f32[4096]{0:T(1024)S(1)} %negate_select_fusion, f32[]{:T(128)} %constant.9.clone.1), kind=kCustom, calls=%fused_computation.15 | custom fusion | flops 3276800 | bytes 13123588 | tf_op jit(solution)/shard_map/scatter-add | solution.py:73
  307.0 31.9 %scatter_fusion = f32[4096,400]{1,0:T(8,128)} fusion(f32[4096,400]{1,0:T(8,128)} %scatter_custom_fusion, s32[4000]{0:T(1024)S(1)} %bitcast.58, f32[4000,400]{1,0:T(8,128)} %reshape.304), kind=kCustom, calls=%fused_computation.5 | custom fusion | flops 1600000 | bytes 19216000 | tf_op jit(solution)/shard_map/scatter-add | solution.py:75
  339.0 69.6 %all-reduce.2.cloned.1.call-done = f32[4096,400]{1,0:T(8,128)} async-done(((f32[4096,400]{1,0:T(8,128)}), f32[4096,400]{1,0:T(8,128)}) %all-reduce.2.cloned.1.call-update) | async-done | bytes 6553616 | tf_op jit(solution)/shard_map/psum | solution.py:82
  408.6 4.1 multiply_reduce_fusion
  413.3 99.9 %reduce-scatter.2.cloned.1.call-done = f32[256,400]{1,0:T(8,128)} async-done(((f32[4096,400]{1,0:T(8,128)}), f32[256,400]{1,0:T(8,128)}) %reduce-scatter.2.cloned.1.call-update) | async-done | bytes 409616 | tf_op jit(solution)/shard_map/reduce_scatter | solution.py:74
  514.4 10.0 %divide_subtract_fusion = f32[4096,400]{1,0:T(8,128)} fusion(f32[4096,400]{1,0:T(8,128)} %copy.25, f32[4096,400]{1,0:T(8,128)} %all-reduce.2.cloned.1.call-done, f32[4096]{0:T(1024)S(1)} %get-tuple-element.12), kind=kLoop, calls=%fused_computation.9 | loop fusion | flops 4915200 | bytes 19677184 | tf_op jit(solution)/shard_map/sub | solution.py:84
  524.4 8.5 %copy.37 = f32[4096,400]{0,1:T(8,128)} copy(f32[4096,400]{1,0:T(8,128)} %divide_subtract_fusion) | data formatting | bytes 13107200
  532.9 26.6 %scatter_custom_fusion.2 = f32[256,400]{1,0:T(8,128)S(1)} fusion(f32[256,400]{1,0:T(8,128)S(1)} %collective-permute-done.1, s32[4096]{0:T(1024)} %bitcast.60, f32[4096,400]{1,0:T(8,128)} %bitcast_add_fusion, f32[4096,400]{1,0:T(8,128)} %gather_fusion.1), kind=kCustom, calls=%fused_computation.13 | custom fusion | flops 3276800 | bytes 17186816 | tf_op jit(solution)/shard_map/scatter-add | solution.py:65
  (54 shorter events, 7.3 us)
Async XLA Ops:
  7.2 94.6 %all-gather.2.cloned.1.call-start = ((), (), s32[]{:S(2)}) async-start(), calls=%async_computation.1 | async-start | bytes 8912896 | tf_op jit(solution)/shard_map/all_gather | solution.py:46
  8.4 35.8 %copy-start = (f32[1,256,400]{2,1,0:T(8,128)}, f32[1,256,400]{2,1,0:T(8,128)S(1)}, u32[]{:S(2)}) copy-start(f32[1,256,400]{2,1,0:T(8,128)S(1)} %copy.24) | copy-start | bytes 1228804
  8.4 16.2 %collective-permute-start = (f32[256,400]{1,0:T(8,128)S(1)}, f32[256,400]{1,0:T(8,128)S(1)}, u32[]{:S(2)}, u32[]{:S(2)}) collective-permute-start(f32[256,400]{1,0:T(8,128)S(1)} %bitcast.52), channel_id=1, source_target_pairs={{0,112},{16,0},{32,16},{48,32},{64,48},{80,64},{96,80},{112,96},{1... | collective-permute-start | bytes 1228808 | tf_op jit(solution)/shard_map/ppermute | solution.py:15
  24.6 0.8 copy-start.3
  25.4 383.1 %all-reduce.2.cloned.1.call-start = ((), (), s32[]{:S(2)}) async-start(), calls=%async_computation.3 | async-start | bytes 16777216 | tf_op jit(solution)/shard_map/psum | solution.py:82
  26.9 0.6 copy-start.4
  44.2 8.6 %copy-start.5 = (s32[1,4096]{1,0:T(1,128)S(1)}, s32[1,4096]{1,0:T(1,128)}, u32[]{:S(2)}) copy-start(s32[1,4096]{1,0:T(1,128)} %param.20) | copy-start | bytes 49156
  52.8 21.5 %copy-start.6 = (s32[1,4000]{1,0:T(1,128)S(1)}, s32[1,4000]{1,0:T(1,128)}, u32[]{:S(2)}) copy-start(s32[1,4000]{1,0:T(1,128)} %param.19) | copy-start | bytes 48004
  52.8 21.5 %copy-start.7 = (s32[1,4000,1]{1,2,0:T(1,128)S(1)}, s32[1,4000,1]{1,2,0:T(1,128)}, u32[]{:S(2)}) copy-start(s32[1,4000,1]{1,2,0:T(1,128)} %param.18) | copy-start | bytes 48004
  52.8 21.5 %copy-start.8 = (s32[1,4096]{1,0:T(1,128)S(1)}, s32[1,4096]{1,0:T(1,128)}, u32[]{:S(2)}) copy-start(s32[1,4096]{1,0:T(1,128)} %param.17) | copy-start | bytes 49156
  52.9 21.5 %copy-start.9 = (s32[1,4096,1]{1,2,0:T(1,128)S(1)}, s32[1,4096,1]{1,2,0:T(1,128)}, u32[]{:S(2)}) copy-start(s32[1,4096,1]{1,2,0:T(1,128)} %param.16) | copy-start | bytes 49156
  151.4 61.5 %slice-start = ((s8[8388608]{0:T(1024)(128)(4,1)}), s8[4194304]{0:T(1024)(128)(4,1)S(1)}, s32[]{:S(2)}) async-start(s8[8388608]{0:T(1024)(128)(4,1)} %bitcast.56), calls=%async_computation.4 | async-start | bytes 8388608
  160.4 32.6 %copy-start.2 = (f32[4096,400]{1,0:T(8,128)}, f32[4096,400]{1,0:T(8,128)S(1)}, u32[]{:S(2)}) copy-start(f32[4096,400]{1,0:T(8,128)S(1)} %get-tuple-element.15) | copy-start | bytes 19660804
  160.4 52.5 %slice-start.1 = ((s8[8388608]{0:T(1024)(128)(4,1)}), s8[4194304]{0:T(1024)(128)(4,1)S(1)}, s32[]{:S(2)}) async-start(s8[8388608]{0:T(1024)(128)(4,1)} %bitcast.56), calls=%async_computation.5 | async-start | bytes 8388608
  249.2 264.0 %reduce-scatter.2.cloned.1.call-start = ((), (), s32[]{:S(2)}) async-start(), calls=%async_computation.2 | async-start | bytes 8912896 | tf_op jit(solution)/shard_map/reduce_scatter | solution.py:74
  339.0 73.7 %copy-start.10 = (f32[4096]{0:T(1024)S(1)}, f32[4096]{0:T(1024)}, u32[]{:S(2)}) copy-start(f32[4096]{0:T(1024)} %param.14) | copy-start | bytes 49156
  513.1 19.8 %collective-permute-start.1 = (f32[256,400]{1,0:T(8,128)}, f32[256,400]{1,0:T(8,128)S(1)}, u32[]{:S(2)}, u32[]{:S(2)}) collective-permute-start(f32[256,400]{1,0:T(8,128)} %reduce-scatter.2.cloned.1.call-done), channel_id=1, source_target_pairs={{0,16},{16,32},{32,48},{48,64},{64,80},{80,96},{96,112},{112,0},{1... | collective-permute-start | bytes 1228808 | tf_op jit(solution)/shard_map/ppermute | solution.py:15
  532.9 26.7 %copy-start.11 = (f32[1,256]{1,0:T(1,128)S(1)}, f32[1,256]{1,0:T(1,128)}, u32[]{:S(2)}) copy-start(f32[1,256]{1,0:T(1,128)} %param.12) | copy-start | bytes 3076
  532.9 26.8 %copy-start.1 = (f32[1,256,400]{2,1,0:T(8,128)S(1)}, f32[1,256,400]{2,1,0:T(8,128)}, u32[]{:S(2)}) copy-start(f32[1,256,400]{2,1,0:T(8,128)} %copy-done) | copy-start | bytes 1228804
Sparse Core Ops, SparseCore 0:
  25.5 76.1 all-gather.1
  249.3 159.2 all-reduce.1
  413.4 99.6 reduce-scatter.1
where the time goes:
time: 577 us; the launch traced here: 568 us
  waiting for transfers between devices  207 us (36%)
  other arithmetic  151 us (26%)
  local copies, waits for them, and re-layouts  116 us (20%)
  matrix products  71.9 us (12%)
  between operations  14.9 us (3%)
  starting transfers between devices  6.95 us (1%)
    reduce_scatter x1, waiting for transfers between devices, on_device(): lax.psum_scatter(term.at[local_n].add(grad_neg, mode='drop'), 'member', s...  99.9 us
    psum x1, waiting for transfers between devices, on_device(): rel_total = lax.psum(rel_grad, ('group', 'member'))  69.6 us
    dot_general x1, matrix products, on_device(): jnp.einsum('cjd,cnd->cjn', query_c, neg_vec, precision=lax.Precision.HIGH...  32.6 us
    scatter-add x1, other arithmetic, on_device(): term.at[local_n].add(grad_neg, mode='drop')  31.9 us
    scatter-add x1, other arithmetic, on_device(): term = term.at[local_r].add(grad_right, mode='drop')  31.1 us
    scatter-add x1, other arithmetic, on_device(): jnp.zeros(relations.shape, jnp.float32).at[rid].add(grad_query * left_vec)  30.1 us
    all_gather x1, waiting for transfers between devices, on_device(): slab = lax.all_gather(right, 'member', axis=0, tiled=True)  27.3 us
    scatter-add x1, other arithmetic, on_device(): jnp.zeros((rows, width), jnp.float32).at[lhs].add(grad_query * rel_vec)  26.6 us
  transfers between devices with their start and end apart: 5, of which 4 were waited for; matrix products, arithmetic and copies ran while one was open for 28% of the time, Pallas kernels for 0%

commit v1 on v0

v1 whole, which is shorter than its diff:
```python
import functools
import jax
import jax.numpy as jnp
from jax import lax
from jax.experimental import pallas as pl
from jax.experimental.pallas import tpu as pltpu
from jax.sharding import PartitionSpec as P

SPAN = 512
NEG = 500
STEP_SIZE = 0.1
LANES = 128
F32 = jnp.float32
BF16 = jnp.bfloat16


def split(x):
    hi = x.astype(BF16)
    return hi, (x - hi.astype(F32)).astype(BF16)


def dot2(a, b, dims):
    return lax.dot_general(a, b, (dims, ((), ())), preferred_element_type=F32)


def dot3(a, b, dims):
    ah, al = a
    bh, bl = b
    return dot2(ah, bh, dims) + (dot2(ah, bl, dims) + dot2(al, bh, dims))


def row(i, chunks):
    return pl.ds(pl.multiple_of(i * chunks, chunks), chunks)


def read_rows(ref, rows, chunks):
    return jnp.concatenate([ref[pl.ds(c, rows, stride=chunks), :] for c in range(chunks)], axis=1)


def write_rows(ref, value, rows, chunks):
    for c in range(chunks):
        ref[pl.ds(c, rows, stride=chunks), :] = value[:, c * LANES : (c + 1) * LANES]


def bucket_kernel(
    spans, chunks, unroll,
    cnt_ref, ridx_ref, nidx_ref, rid_ref, lhs_ref, ent_ref, rel_ref, slab_hbm,
    right_hbm, relg_hbm, left_ref,
    slab, racc, nacc, relacc, rvec, nvec, gr, gn, grel, sem,
):
    s = pl.program_id(0)
    rows = racc.shape[0] // chunks

    @pl.when(s == 0)
    def _():
        load = pltpu.make_async_copy(slab_hbm, slab.at[pl.ds(0, rows * chunks)], sem.at[0])
        load.start()
        slab[pl.ds(rows * chunks, 8), :] = jnp.zeros((8, LANES), F32)
        racc[...] = jnp.zeros_like(racc)
        nacc[...] = jnp.zeros_like(nacc)
        relacc[...] = jnp.zeros_like(relacc)
        left_ref[...] = jnp.zeros_like(left_ref)
        gr[...] = jnp.zeros_like(gr)
        gn[...] = jnp.zeros_like(gn)
        grel[...] = jnp.zeros_like(grel)
        load.wait()

    def scatter(j, base):
        rel = row(rid_ref[base + j], chunks)
        rgt = row(ridx_ref[base + j], chunks)
        neg = row(nidx_ref[base + j], chunks)
        own = row(j, chunks)
        relacc[rel, :] = relacc[rel, :] + grel[own, :]
        racc[rgt, :] = racc[rgt, :] + gr[own, :]
        nacc[neg, :] = nacc[neg, :] + gn[own, :]

    def gather(j, base):
        own = row(j, chunks)
        rvec[own, :] = slab[row(ridx_ref[base + j], chunks), :]
        nvec[own, :] = slab[row(nidx_ref[base + j], chunks), :]

    behind = jnp.maximum(s - 1, 0) * SPAN
    ahead = jnp.minimum(s, spans - 1) * SPAN

    def step(b, carry):
        for u in range(unroll):
            j = b * unroll + u
            gather(j, ahead)
            scatter(j, behind)
        return carry

    lax.fori_loop(0, SPAN // unroll, step, 0)

    @pl.when(s < spans)
    def _():
        hot = (lax.broadcasted_iota(jnp.int32, (ent_ref.shape[0], SPAN), 0) == lhs_ref[0]).astype(F32).astype(BF16)
        eh, el = split(ent_ref[...])
        first = ((0,), (0,))
        last = ((1,), (1,))
        inner = ((1,), (0,))
        left = dot2(hot, eh, first) + dot2(hot, el, first)
        rel = rel_ref[...]
        query = left * rel
        live = (s * SPAN + lax.broadcasted_iota(jnp.int32, (SPAN, 1), 0) < cnt_ref[0]).astype(F32)
        q = split(query)
        n = split(read_rows(nvec, SPAN, chunks))
        neg = dot3(q, n, last)
        dneg = split(jax.nn.sigmoid(neg) * (live / NEG))
        right = read_rows(rvec, SPAN, chunks)
        pos = jnp.sum(query * right, axis=1, keepdims=True)
        dpos = -jax.nn.sigmoid(-pos) * live
        write_rows(gr, dpos * query, SPAN, chunks)
        write_rows(gn, dot3(dneg, q, first), SPAN, chunks)
        grad_query = dpos * right + dot3(dneg, n, inner)
        write_rows(grel, grad_query * left, SPAN, chunks)
        gl = split(grad_query * rel)
        left_ref[...] += dot2(hot, gl[0], inner) + dot2(hot, gl[1], inner)

    @pl.when(s == spans)
    def _():
        out_rel = pltpu.make_async_copy(relacc, relg_hbm, sem.at[0])
        out_rel.start()
        tile = 2048

        def add(i, carry):
            part = pl.ds(pl.multiple_of(i * tile, tile), tile)
            racc[part, :] = racc[part, :] + nacc[part, :]
            return carry

        lax.fori_loop(0, rows * chunks // tile, add, 0)
        out_right = pltpu.make_async_copy(racc, right_hbm, sem.at[1])
        out_right.start()
        out_rel.wait()
        out_right.wait()


def bucket(counts, ridx, nidx, rid, lhs, ent, rel_rows, slab):
    edges, width = rel_rows.shape
    chunks = width // LANES
    spans = edges // SPAN
    rows = slab.shape[0] // chunks
    smem = pl.BlockSpec(memory_space=pltpu.SMEM)
    anym = pl.BlockSpec(memory_space=pl.ANY)
    vm = lambda r: pltpu.VMEM((r * chunks, LANES), F32)
    return pl.pallas_call(
        functools.partial(bucket_kernel, spans, chunks, 8),
        grid=(spans + 1,),
        out_shape=(
            jax.ShapeDtypeStruct((rows * chunks, LANES), F32),
            jax.ShapeDtypeStruct((rows * chunks, LANES), F32),
            jax.ShapeDtypeStruct(ent.shape, F32),
        ),
        in_specs=[
            smem, smem, smem, smem,
            pl.BlockSpec((1, 1, SPAN), lambda s: (jnp.minimum(s, spans - 1), 0, 0)),
            pl.BlockSpec(ent.shape, lambda s: (0, 0)),
            pl.BlockSpec((SPAN, width), lambda s: (jnp.minimum(s, spans - 1), 0)),
            anym,
        ],
        out_specs=(anym, anym, pl.BlockSpec(ent.shape, lambda s: (0, 0))),
        scratch_shapes=[
            vm(rows + 2), vm(rows), vm(rows + 2), vm(rows),
            vm(SPAN), vm(SPAN), vm(SPAN), vm(SPAN), vm(SPAN),
            pltpu.SemaphoreType.DMA((2,)),
        ],
        compiler_params=pltpu.CompilerParams(vmem_limit_bytes=58 * 2**20),
        name="bucket",
    )(counts, ridx, nidx, rid, lhs, ent, rel_rows, slab)


def from_behind(array, axis, by):
    devices = lax.axis_size(axis)
    return lax.ppermute(array, axis, [(i, (i + by) % devices) for i in range(devices)])


def on_device(
    entities, ent_state, relations, rel_state, lhs_rows, rhs_owner, rhs_off, neg_owner, neg_off, rel_ids, counts
):
    shard = entities[0]
    rows, width = shard.shape
    wide = -(-width // LANES) * LANES
    chunks = wide // LANES
    members = lax.axis_size("member")
    padded = jnp.pad(shard, ((0, 0), (0, wide - width)))
    right = from_behind(padded.reshape(rows * chunks, LANES), "group", -1)
    slab = lax.all_gather(right, "member", axis=0, tiled=True)
    edges = lhs_rows.shape[1]
    spans = edges // SPAN
    ridx = rhs_owner[0, :, 0] * rows + rhs_off[0]
    nidx = (neg_owner[0, :, 0] * rows + neg_off[0]).reshape(spans, NEG)
    nidx = jnp.pad(nidx, ((0, 0), (0, SPAN - NEG)), constant_values=rows * members).reshape(edges)
    rid = rel_ids[0]
    rel_rows = jnp.pad(relations, ((0, 0), (0, wide - width)))[rid]
    right_part, rel_part, left_grad = bucket(
        counts[0], ridx, nidx, rid, lhs_rows.reshape(spans, 1, SPAN), padded, rel_rows, slab
    )
    right_grad = lax.psum_scatter(right_part, "member", scatter_dimension=0, tiled=True)
    returned = from_behind(right_grad, "group", 1).reshape(rows, wide)
    grad_total = (left_grad + returned)[:, :width]
    new_state = ent_state[0] + jnp.mean(grad_total * grad_total, axis=1)
    new_shard = shard - STEP_SIZE * grad_total / jnp.sqrt(new_state)[:, None]
    rel_total = lax.psum(rel_part, ("group", "member")).reshape(-1, wide)[:, :width]
    rel_new_state = rel_state + jnp.mean(rel_total * rel_total, axis=1)
    rel_new = relations - STEP_SIZE * rel_total / jnp.sqrt(rel_new_state)[:, None]
    return (new_shard[None], new_state[None], rel_new, rel_new_state)


def solution(mesh):
    in_specs = (
        P("group", "member", None), P("group", "member"), P(), P(),
        P("group", "member"), P("group", "member", None), P("group", "member"),
        P("group", "member", None), P("group", "member"), P("group", "member"), P("group", "member"),
    )
    out_specs = (P("group", "member", None), P("group", "member"), P(), P())
    return jax.shard_map(on_device, mesh=mesh, in_specs=in_specs, out_specs=out_specs, check_vma=False)
```

time: 577 us -> 478 us (0.83); the launches traced: 568 us -> 476 us
  other arithmetic: 151 us -> 17.4 us
  waiting for transfers between devices: 207 us -> 307 us
  matrix products: 71.9 us -> 0 us
  Pallas kernels: 0 us -> 69.6 us
  local copies, waits for them, and re-layouts: 116 us -> 60.6 us
    scatter-add x4 -> x0, other arithmetic: 120 us -> none  [the longest x1 31.9 us: on_device(): term.at[local_n].add(grad_neg, mode='drop')]
    psum x1, waiting for transfers between devices: 69.6 us -> 159 us  [on_device(): lax.psum(rel_part, ('group', 'member')).reshape(-1, wide)[:, :width]]
    pallas_call x0 -> x1, Pallas kernels: none -> 69.6 us  [bucket(): pl.pallas_call(functools.partial(bucket_kernel, spans, chunks, 8), grid=(...]
    gather x4 -> x2, local copies, waits for them, and re-layouts: 80.8 us -> 29.3 us  [on_device(): rel_rows = jnp.pad(relations, ((0, 0), (0, wide - width)))[rid]]
    reshape x2 -> x0, matrix products: 39.3 us -> none  [the longest x1 19.9 us: on_device(): grad_query = dpos[:, None] * right_vec + jnp.einsum('cjn,cnd->cjd', dneg,...]
    dot_general x1 -> x0, matrix products: 32.6 us -> none  [on_device(): jnp.einsum('cjd,cnd->cjn', query_c, neg_vec, precision=lax.Precision.HIGH...]
    reduce_sum x1 -> x0, other arithmetic: 9.01 us -> none  [on_device(): pos = jnp.sum(query * right_vec, axis=1)]
    unnamed x32 -> x22, local copies, waits for them, and re-layouts: 20.7 us -> 12.7 us
  transfers between devices with their start and end apart: 5 -> 5, of which waited for: 4 -> 5; matrix products, arithmetic and copies ran while one was open for 28% -> 12% of each run, Pallas kernels for 0% -> 0%
where the time goes in v1:
time: 478 us; the launch traced here: 476 us
  waiting for transfers between devices  307 us (64%)
  Pallas kernels  69.6 us (15%)
  local copies, waits for them, and re-layouts  60.6 us (13%)
  other arithmetic  17.4 us (4%)
  between operations  14.6 us (3%)
  starting transfers between devices  6.95 us (1%)
    psum x1, waiting for transfers between devices, on_device(): lax.psum(rel_part, ('group', 'member')).reshape(-1, wide)[:, :width]  159 us
    reduce_scatter x1, waiting for transfers between devices, on_device(): lax.psum_scatter(right_part, 'member', scatter_dimension=0, tiled=True)  100 us
    pallas_call x1, Pallas kernels, bucket(): pl.pallas_call(functools.partial(bucket_kernel, spans, chunks, 8), grid=(...  69.6 us
    all_gather x1, waiting for transfers between devices, on_device(): slab = lax.all_gather(right, 'member', axis=0, tiled=True)  33.6 us
    gather x2, local copies, waits for them, and re-layouts, on_device(): rel_rows = jnp.pad(relations, ((0, 0), (0, wide - width)))[rid]  29.3 us
    reshape x2, local copies, waits for them, and re-layouts, on_device(): lax.psum(rel_part, ('group', 'member')).reshape(-1, wide)[:, :width]  18.3 us
    ppermute x2, waiting for transfers between devices, from_behind(): lax.ppermute(array, axis, [(i, (i + by) % devices) for i in range(devices)])  13.9 us
    unnamed x22, local copies, waits for them, and re-layouts  12.7 us
  transfers between devices with their start and end apart: 5, of which 5 were waited for; matrix products, arithmetic and copies ran while one was open for 12% of the time, Pallas kernels for 0%

profile of v1, /device:TPU:1, one launch (start us, length us, event | category | flops | bytes accessed | tf_op | source)
XLA Modules:
  0.0 476.4 jit_solution(1828052318492465880)
XLA Ops:
  7.2 1.2 copy.19
  8.5 5.6 %collective-permute-start = (f32[1024,128]{1,0:T(8,128)S(1)}, f32[1024,128]{1,0:T(8,128)S(1)}, u32[]{:S(2)}, u32[]{:S(2)}) collective-permute-start(f32[1024,128]{1,0:T(8,128)S(1)} %reshape.79), channel_id=1, source_target_pairs={{0,112},{16,0},{32,16},{48,32},{64,48},{80,64},{96,80},{112,96},{1... | collective-permute-start | bytes 1572872 | tf_op jit(solution)/shard_map/ppermute | solution.py:173
  14.1 10.6 %collective-permute-done = f32[1024,128]{1,0:T(8,128)S(1)} collective-permute-done((f32[1024,128]{1,0:T(8,128)S(1)}, f32[1024,128]{1,0:T(8,128)S(1)}, u32[]{:S(2)}, u32[]{:S(2)}) %collective-permute-start) | collective-permute-done | bytes 524320 | tf_op jit(solution)/shard_map/ppermute | solution.py:173
  24.7 0.9 copy-done.2
  26.8 1.4 reduce.7
  28.3 0.8 multiply_reduce_fusion.2
  29.2 0.6 copy.23
  29.8 8.5 %copy.20 = f32[4096,400]{1,0:T(8,128)} copy(f32[4096,400]{0,1:T(8,128)} %param.13) | data formatting | bytes 13107200 | tf_op args[2]
  38.4 21.7 %gather_fusion = f32[4096,400]{1,0:T(8,128)} fusion(f32[4096,400]{1,0:T(8,128)} %copy.20, s32[4096]{0:T(1024)S(1)} %broadcast_clamp_fusion), kind=kCustom, calls=%fused_computation | custom fusion | bytes 13123584 | tf_op jit(solution)/shard_map/gather | solution.py:193
  60.1 7.6 %gather.7.rel_ref = f32[4096,512]{1,0:T(8,128)} pad(f32[4096,400]{1,0:T(8,128)} %gather_fusion, f32[]{:T(128)} %constant.8.clone.1), padding=0_0x0_112 | pad | bytes 14942212 | tf_op jit(solution)/shard_map/gather | solution.py:193
  67.7 0.6 add.46.ridx_ref
  68.3 33.6 %all-gather.2.cloned.1.call-done.slab_hbm = f32[16384,128]{1,0:T(8,128)} async-done(((f32[1024,128]{1,0:T(8,128)}), f32[16384,128]{1,0:T(8,128)}) %all-gather.2.cloned.1.call-update) | async-done | bytes 8388624 | tf_op jit(solution)/shard_map/all_gather | solution.py:186
  101.9 69.6 %bucket.1 = (f32[16384,128]{1,0:T(8,128)}, f32[16384,128]{1,0:T(8,128)}, f32[256,512]{1,0:T(8,128)}) custom-call(s32[1]{0:T(128)} %bitcast.17.cnt_ref, s32[4096]{0:T(1024)} %add.46.ridx_ref, s32[4096]{0:T(1024)} %bitcast.20, s32[4096]{0:T(1024)} %bitcast.19, s32[8,1,512]{2,1,0:T(1,128)} %bitcast.23, f32[256,512]{1,0:T(8,128)} %copy-done, ...), custom_call_target="tpu_custom_call" | custom-call | tf_op jit(solution)/shard_map/bucket/pallas_call | solution.py:145
  171.5 9.3 %reshape.81 = f32[4096,512]{1,0:T(8,128)} reshape(f32[16384,128]{1,0:T(8,128)} %get-tuple-element.9) | data formatting | bytes 16777216 | tf_op jit(solution)/shard_map/reshape | solution.py:202
  180.8 8.9 %copy.21 = f32[4096,512]{0,1:T(8,128)} copy(f32[4096,512]{1,0:T(8,128)} %reshape.81) | data formatting | bytes 16777216 | tf_op jit(solution)/shard_map/reshape | solution.py:202
  189.8 0.7 reduce-scatter.2.cloned.1.call-update
  190.5 158.7 %all-reduce.5.cloned.1.call-done = f32[4096,512]{0,1:T(8,128)} async-done(((f32[4096,512]{0,1:T(8,128)}), f32[4096,512]{0,1:T(8,128)}) %all-reduce.5.cloned.1.call-update) | async-done | bytes 8388624 | tf_op jit(solution)/shard_map/psum | solution.py:202
  349.2 3.5 multiply_reduce_fusion
  352.7 0.6 fusion
  353.3 100.5 %reduce-scatter.2.cloned.1.call-done = f32[1024,128]{1,0:T(8,128)} async-done(((f32[16384,128]{1,0:T(8,128)}), f32[1024,128]{1,0:T(8,128)}) %reduce-scatter.2.cloned.1.call-update) | async-done | bytes 524304 | tf_op jit(solution)/shard_map/reduce_scatter | solution.py:197
  453.8 1.2 collective-permute-start.1
  455.0 9.6 %divide_subtract_fusion = f32[4096,400]{0,1:T(8,128)} fusion(f32[4096,400]{0,1:T(8,128)} %param.13, f32[4096,512]{0,1:T(8,128)} %all-reduce.5.cloned.1.call-done, f32[4096]{0:T(1024)S(1)} %get-tuple-element.18), kind=kLoop, calls=%fused_computation.1 | loop fusion | flops 4915200 | bytes 19677184 | tf_op jit(solution)/shard_map/sub | solution.py:204
  464.6 3.3 collective-permute-done.1
  468.3 0.9 copy.22
  (35 shorter events, 2.0 us)
Async XLA Ops:
  7.2 94.7 %all-gather.2.cloned.1.call-start = ((), (), s32[]{:S(2)}) async-start(), calls=%async_computation.1 | async-start | bytes 8912896 | tf_op jit(solution)/shard_map/all_gather | solution.py:186
  8.5 29.9 %copy-start = (f32[256,512]{1,0:T(8,128)}, f32[256,512]{1,0:T(8,128)S(1)}, u32[]{:S(2)}) copy-start(f32[256,512]{1,0:T(8,128)S(1)} %pad.12.ent_ref) | copy-start | bytes 1572868
  8.5 29.8 %copy-start.3 = (s32[1,4096]{1,0:T(1,128)S(1)}, s32[1,4096]{1,0:T(1,128)}, u32[]{:S(2)}) copy-start(s32[1,4096]{1,0:T(1,128)} %param.20) | copy-start | bytes 49156
  8.5 16.2 %collective-permute-start = (f32[1024,128]{1,0:T(8,128)S(1)}, f32[1024,128]{1,0:T(8,128)S(1)}, u32[]{:S(2)}, u32[]{:S(2)}) collective-permute-start(f32[1024,128]{1,0:T(8,128)S(1)} %reshape.79), channel_id=1, source_target_pairs={{0,112},{16,0},{32,16},{48,32},{64,48},{80,64},{96,80},{112,96},{1... | collective-permute-start | bytes 1572872 | tf_op jit(solution)/shard_map/ppermute | solution.py:173
  24.7 0.9 copy-start.2
  25.6 323.6 %all-reduce.5.cloned.1.call-start = ((), (), s32[]{:S(2)}) async-start(), calls=%async_computation.3 | async-start | bytes 16777216 | tf_op jit(solution)/shard_map/psum | solution.py:202
  60.1 7.6 %copy-start.5 = (s32[1,4096,1]{1,2,0:T(1,128)S(1)}, s32[1,4096,1]{1,2,0:T(1,128)}, u32[]{:S(2)}) copy-start(s32[1,4096,1]{1,2,0:T(1,128)} %param.16) | copy-start | bytes 49156
  60.1 7.6 %copy-start.4 = (s32[1,4096]{1,0:T(1,128)S(1)}, s32[1,4096]{1,0:T(1,128)}, u32[]{:S(2)}) copy-start(s32[1,4096]{1,0:T(1,128)} %param.17) | copy-start | bytes 49156
  189.8 162.9 %copy-start.6 = (f32[4096]{0:T(1024)S(1)}, f32[4096]{0:T(1024)}, u32[]{:S(2)}) copy-start(f32[4096]{0:T(1024)} %param.14) | copy-start | bytes 49156
  189.8 264.0 %reduce-scatter.2.cloned.1.call-start = ((), (), s32[]{:S(2)}) async-start(), calls=%async_computation.2 | async-start | bytes 8912896 | tf_op jit(solution)/shard_map/reduce_scatter | solution.py:197
  453.8 14.1 %collective-permute-start.1 = (f32[1024,128]{1,0:T(8,128)}, f32[1024,128]{1,0:T(8,128)S(1)}, u32[]{:S(2)}, u32[]{:S(2)}) collective-permute-start(f32[1024,128]{1,0:T(8,128)} %reduce-scatter.2.cloned.1.call-done), channel_id=1, source_target_pairs={{0,16},{16,32},{32,48},{48,64},{64,80},{80,96},{96,112},{112,0},{1... | collective-permute-start | bytes 1572872 | tf_op jit(solution)/shard_map/ppermute | solution.py:173
  455.0 13.0 %copy-start.1 = (f32[256,512]{1,0:T(8,128)S(1)}, f32[256,512]{1,0:T(8,128)}, u32[]{:S(2)}) copy-start(f32[256,512]{1,0:T(8,128)} %get-tuple-element.7) | copy-start | bytes 1572868
  455.0 13.1 %copy-start.7 = (f32[1,256]{1,0:T(1,128)S(1)}, f32[1,256]{1,0:T(1,128)}, u32[]{:S(2)}) copy-start(f32[1,256]{1,0:T(1,128)} %param.12) | copy-start | bytes 3076
Sparse Core Ops, SparseCore 0:
  25.7 76.1 all-gather.1
  189.9 159.2 all-reduce.4
  354.1 99.6 reduce-scatter.1

commit v2 on v1

v2 whole, which is shorter than its diff:
```python
import functools
import jax
import jax.numpy as jnp
from jax import lax
from jax.experimental import pallas as pl
from jax.experimental.pallas import tpu as pltpu
from jax.sharding import PartitionSpec as P

SPAN = 512
NEG = 500
STEP_SIZE = 0.1
LANES = 128
F32 = jnp.float32
BF16 = jnp.bfloat16
MESH = pl.DeviceIdType.MESH

CHUNKS = 4
TAIL = 16
GROUP = 32
PACK = 104
PARTS = 4
PART = 208
BLOCKS = 16
RING = 4
PART_ORDER = (("y", "xhi"), ("xhi", "y"), ("y", "xhi"), ("xhi", "y"))
PIECE_ROWS = (32, 32, 40)
PIECE_SUM = (("z", "y", "x"), ("x", "z", "y"), ("z", "x", "y"))
PIECE_OUT = (("z", "y", "x"), ("x", "z", "y"), ("y", "z", "x"))
SHARDS = 64


def split(x):
    hi = x.astype(BF16)
    return hi, (x - hi.astype(F32)).astype(BF16)


def dot2(a, b, dims):
    return lax.dot_general(a, b, (dims, ((), ())), preferred_element_type=F32)


def dot3(a, b, dims):
    ah, al = a
    bh, bl = b
    return dot2(ah, bh, dims) + (dot2(ah, bl, dims) + dot2(al, bh, dims))


def row(i):
    return pl.ds(pl.multiple_of(i * CHUNKS, CHUNKS), CHUNKS)


def span_of(start, size, tile=8):
    return pl.ds(start if isinstance(start, int) else pl.multiple_of(start, tile), size)


def read_rows(ref, rows):
    return jnp.concatenate([ref[pl.ds(c, rows, stride=CHUNKS), :] for c in range(CHUNKS)], axis=1)


def write_rows(ref, value, rows):
    for c in range(CHUNKS):
        ref[pl.ds(c, rows, stride=CHUNKS), :] = value[:, c * LANES : (c + 1) * LANES]


def pack_tail(tail):
    packed = tail[0:8]
    for g in range(1, GROUP // 8):
        packed = packed + pltpu.roll(tail[8 * g : 8 * g + 8], TAIL * g, 1)
    return packed


def unpack_tail(packed):
    kept = lax.broadcasted_iota(jnp.int32, (8, LANES), 1) < TAIL
    parts = [jnp.where(kept, packed if g == 0 else pltpu.roll(packed, LANES - TAIL * g, 1), 0.0) for g in range(GROUP // 8)]
    return jnp.concatenate(parts, axis=0)


def digits_of(flat, order):
    sizes = {"y": 4, "xhi": 2, "x": 4, "z": 4}
    out = {}
    for name in reversed(order):
        out[name] = flat % sizes[name]
        flat = flat // sizes[name]
    return out


def index_of(where, order):
    sizes = {"y": 4, "xhi": 2, "x": 4, "z": 4}
    at = 0
    for name in order:
        at = at * sizes[name] + where[name]
    return at


def part_row(member, part):
    where = digits_of(member // 2, ("y", "xhi"))
    at = (member % 2) * 8 + index_of(where, PART_ORDER[part])
    return part * BLOCKS * PART + at * PART


def shard_row(group, piece, orders):
    where = digits_of(group % SHARDS, ("z", "y", "x"))
    return ((group // SHARDS) * SHARDS + index_of(where, orders[piece])) * PIECE_ROWS[piece]


def here():
    g = lax.axis_index("group")
    m = lax.axis_index("member")
    return {"x": (m // 2) % 2 * 2 + g // 4, "xhi": (m // 2) % 2, "y": m // 4, "z": g % 4, "core": m % 2}


def device(at):
    return (at["x"] % 2 * 4 + at["z"], at["y"] * 4 + at["x"] // 2 * 2 + at["core"])


def toward(at, axis, step):
    there = dict(at)
    if axis == "core":
        there["core"] = 1 - at["core"]
    elif axis == "xhi":
        there["x"] = (at["x"] + 2) % 4
    else:
        there[axis] = (at[axis] + step + 4) % 4
    return device(there)


def next_group(step):
    return ((lax.axis_index("group") + step + 8) % 8, lax.axis_index("member"))


def greet(devices):
    barrier = pltpu.get_barrier_semaphore()
    for there in devices:
        pl.semaphore_signal(barrier, inc=1, device_id=there, device_id_type=MESH)
    pl.semaphore_wait(barrier, len(devices))


class Copies:
    def __init__(self, send, recv, local):
        self.send, self.recv, self.local = send, recv, local
        self.started, self.kept, self.homes = 0, [], 0

    def to(self, there, src, dst):
        copy = pltpu.make_async_remote_copy(
            src_ref=src, dst_ref=dst, send_sem=self.send.at[self.started], recv_sem=self.recv.at[self.started],
            device_id=there, device_id_type=MESH,
        )
        copy.start()
        self.started += 1
        self.kept.append(copy)
        return copy

    def home(self, src, dst):
        copy = pltpu.make_async_copy(src, dst, self.local.at[self.homes])
        copy.start()
        self.homes += 1
        return copy

    def finish(self):
        for copy in self.kept:
            copy.wait_send()


def merged(flows):
    flows = list(flows)
    while flows:
        left = []
        for flow in flows:
            try:
                next(flow)
            except StopIteration:
                continue
            left.append(flow)
            yield
        flows = left


def run_beside(flows, beside):
    for _ in merged(flows):
        next(beside, None)
    for _ in beside:
        pass


def halves(size):
    first = -(-size // 16) * 8
    return first, size - first


def add_into(dst, at, src, start, size):
    tile = size
    while tile > 256:
        tile = tile // 2 if tile % 16 == 0 else tile // 13
    if tile == size:
        dst[span_of(at, size), :] = dst[span_of(at, size), :] + src[span_of(start, size), :]
        return

    def step(i, carry):
        d = span_of(at + i * tile, tile)
        dst[d, :] = dst[d, :] + src[span_of(start + i * tile, tile), :]
        return carry

    lax.fori_loop(0, size // tile, step, 0)


def sum_flow(net, at, src, acc, landing, ring, order, done):
    half = acc.shape[0]
    core = at["core"]
    over = net.to(toward(at, "core", 1), src.at[span_of((1 - core) * half, half)], landing)
    own = net.home(src.at[span_of(core * half, half)], acc)
    yield
    own.wait()
    over.wait_recv()
    add_into(acc, 0, landing, 0, half)
    base, size, used = 0, half, 0
    for axis in order:
        a = at[axis]
        if axis == "xhi":
            size = size // 2
            copy = net.to(toward(at, axis, 1), acc.at[span_of(base + (1 - a) * size, size)], ring.at[pl.ds(used, size)])
            yield
            copy.wait_recv()
            add_into(acc, base + a * size, ring, used, size)
            used += size
        else:
            size = size // RING
            h1, h2 = halves(size)
            up, down, far = (base + (a + k) % RING * size for k in (1, 3, 2))
            above, below = toward(at, axis, 1), toward(at, axis, -1)
            ra, rb, rc, rd = used, used + h1, used + size, used + 2 * size
            first = net.to(above, acc.at[span_of(far, h1)], ring.at[pl.ds(ra, h1)])
            second = net.to(below, acc.at[span_of(far + h1, h2)], ring.at[pl.ds(rb, h2)])
            c2 = net.to(above, acc.at[span_of(up + h1, h2)], ring.at[pl.ds(rc + h1, h2)])
            d1 = net.to(below, acc.at[span_of(down, h1)], ring.at[pl.ds(rd, h1)])
            yield
            first.wait_recv()
            add_into(acc, up, ring, ra, h1)
            c1 = net.to(above, acc.at[span_of(up, h1)], ring.at[pl.ds(rc, h1)])
            second.wait_recv()
            add_into(acc, down + h1, ring, rb, h2)
            d2 = net.to(below, acc.at[span_of(down + h1, h2)], ring.at[pl.ds(rd + h1, h2)])
            yield
            own = base + a * size
            c2.wait_recv()
            d1.wait_recv()
            c1.wait_recv()
            d2.wait_recv()
            add_into(acc, own, ring, rc, size)
            add_into(acc, own, ring, rd, size)
            used += 3 * size
        base = base + a * size
    yield from done(base)


def spread_flow(net, at, buf, offset, rows, order, arrived):
    radix = {"xhi": 2, "x": 4, "y": 4, "z": 4}
    total = rows
    for name in order:
        total *= radix[name]
    core = at["core"]
    bases = [offset + core * total]
    strides = []
    size = total
    for name in order:
        size = size // radix[name]
        strides.append(size)
        bases.append(bases[-1] + at[name] * size)
    sibling = toward(at, "core", 1)
    shared = []

    def share(start, size):
        there = span_of(start, size)
        shared.append((net.to(sibling, buf.at[there], buf.at[there]), start + (1 - 2 * core) * total, size))
        arrived(start, size)

    for level in reversed(range(len(order))):
        name, size, region = order[level], strides[level], bases[level]
        a = at[name]
        last = level == 0
        own = span_of(region + a * size, size)
        if name == "xhi":
            copy = net.to(toward(at, name, 1), buf.at[own], buf.at[own])
            if last:
                share(region + a * size, size)
            yield
            copy.wait_recv()
            if last:
                share(region + (1 - a) * size, size)
        else:
            h1, h2 = halves(size)
            up, down, far = (region + (a + k) % RING * size for k in (1, 3, 2))
            above, below = toward(at, name, 1), toward(at, name, -1)
            e = net.to(above, buf.at[own], buf.at[own])
            f = net.to(below, buf.at[own], buf.at[own])
            if last:
                share(region + a * size, size)
            yield
            e.wait_recv()
            lower = span_of(down, h1)
            g = net.to(above, buf.at[lower], buf.at[lower])
            f.wait_recv()
            upper = span_of(up + h1, h2)
            h = net.to(below, buf.at[upper], buf.at[upper])
            if last:
                share(down, size)
                share(up, size)
            yield
            g.wait_recv()
            h.wait_recv()
            if last:
                share(far, size)
    yield
    for copy, start, size in shared:
        copy.wait_recv()
        arrived(start, size)


def fetch_kernel(rid_ref, ent_ref, rel_hbm, slab_hbm, rows_hbm, own, packed, slab, rel, rel_rows, got, send, recv, local):
    at = here()
    m = lax.axis_index("member")
    greet(
        [toward(at, "y", 1), toward(at, "y", -1), toward(at, "xhi", 1), toward(at, "core", 1), next_group(1), next_group(-1)]
    )
    net = Copies(send, recv, local)
    entry = net.home(rel_hbm, rel)
    for j in range(8):
        rows = slice(j * GROUP, (j + 1) * GROUP)
        for c in range(3):
            own[pl.ds(j * PACK + c * GROUP, GROUP), :] = ent_ref[rows, c * LANES : (c + 1) * LANES]
        own[pl.ds(j * PACK + 96, 8), :] = pack_tail(ent_ref[rows, 3 * LANES : 4 * LANES])

    writes = []

    def flow(part):
        start = part * BLOCKS * PART
        mine = span_of(part_row(m, part), PART)
        shift = net.to(next_group(-1), own.at[pl.ds(part * PART, PART)], packed.at[mine])
        yield
        shift.wait_recv()

        def arrived(begin, size):
            def block(i, carry):
                source = begin + i * PART
                flat = (source - start) // PART
                where = digits_of(flat % 8, PART_ORDER[part])
                member = (where["y"] * 2 + where["xhi"]) * 2 + flat // 8
                for half in range(2):
                    base = source + half * PACK
                    out = (member * 256 + part * 64 + half * GROUP) * CHUNKS
                    out = pl.multiple_of(out, 128)
                    for c in range(3):
                        slab[pl.ds(out + c, GROUP, stride=CHUNKS), :] = packed[span_of(base + c * GROUP, GROUP), :]
                    slab[pl.ds(out + 3, GROUP, stride=CHUNKS), :] = unpack_tail(packed[span_of(base + 96, 8), :])
                return carry

            lax.fori_loop(0, size // PART, block, 0)

        yield from spread_flow(net, at, packed, start, PART, PART_ORDER[part], arrived)

    def gather():
        tile = 256
        width, total = rel.shape
        entry.wait()
        for t in range(total // (4 * tile)):
            def convert(i, carry):
                k = t * 4 + i
                part = span_of(k * tile, tile, tile)
                wide = jnp.concatenate([rel[:, part], jnp.zeros((CHUNKS * LANES - width, tile), F32)], axis=0)
                rel_rows[part] = wide.T.reshape(tile, CHUNKS, LANES)
                return carry

            lax.fori_loop(0, 4, convert, 0)
            yield
        edges = got.shape[0] // CHUNKS
        segment, unroll = 512, 16
        for t in range(edges // segment):
            def step(b, carry):
                for u in range(unroll):
                    j = t * segment + b * unroll + u
                    got[row(j), :] = rel_rows[rid_ref[j]]
                return carry

            lax.fori_loop(0, segment // unroll, step, 0)
            part = pl.ds(t * segment * CHUNKS, segment * CHUNKS)
            writes.append(net.home(got.at[part], rows_hbm.at[part]))
            yield

    run_beside([flow(part) for part in range(PARTS)], gather())
    writes.append(net.home(slab, slab_hbm))
    for write in writes:
        write.wait()
    net.finish()


def fetch(rid, ent, relations):
    edges = rid.shape[0]
    width, count = relations.shape
    rows = ent.shape[0] * BLOCKS
    anym = pl.BlockSpec(memory_space=pl.ANY)
    return pl.pallas_call(
        fetch_kernel,
        out_shape=(
            jax.ShapeDtypeStruct((rows * CHUNKS, LANES), F32),
            jax.ShapeDtypeStruct((edges * CHUNKS, LANES), F32),
        ),
        in_specs=[pl.BlockSpec(memory_space=pltpu.SMEM), pl.BlockSpec(memory_space=pltpu.VMEM), anym],
        out_specs=(anym, anym),
        scratch_shapes=[
            pltpu.VMEM((PARTS * PART, LANES), F32),
            pltpu.VMEM((PARTS * BLOCKS * PART, LANES), F32),
            pltpu.VMEM((rows * CHUNKS, LANES), F32),
            pltpu.VMEM((width, count), F32),
            pltpu.VMEM((count, CHUNKS, LANES), F32),
            pltpu.VMEM((edges * CHUNKS, LANES), F32),
            pltpu.SemaphoreType.DMA((96,)),
            pltpu.SemaphoreType.DMA((96,)),
            pltpu.SemaphoreType.DMA((16,)),
        ],
        compiler_params=pltpu.CompilerParams(vmem_limit_bytes=56 * 2**20, collective_id=1, has_side_effects=True),
        name="fetch",
    )(rid, ent, relations)


def bucket_kernel(
    spans, unroll,
    cnt_ref, ridx_ref, nidx_ref, rid_ref, lhs_ref, ent_ref, rel_ref, slab_hbm,
    right_hbm, rel0_hbm, rel1_hbm, rel2_hbm, left_ref,
    slab, racc, nacc, relacc, rvec, nvec, gr, gn, grel, sem,
):
    s = pl.program_id(0)
    total = racc.shape[0]

    @pl.when(s == 0)
    def _():
        load = pltpu.make_async_copy(slab_hbm, slab.at[pl.ds(0, total)], sem.at[0])
        load.start()
        slab[pl.ds(total, 8), :] = jnp.zeros((8, LANES), F32)
        racc[...] = jnp.zeros_like(racc)
        nacc[...] = jnp.zeros_like(nacc)
        relacc[...] = jnp.zeros_like(relacc)
        left_ref[...] = jnp.zeros_like(left_ref)
        gr[...] = jnp.zeros_like(gr)
        gn[...] = jnp.zeros_like(gn)
        grel[...] = jnp.zeros_like(grel)
        load.wait()

    def scatter(j, base):
        rel = row(rid_ref[base + j])
        rgt = row(ridx_ref[base + j])
        neg = row(nidx_ref[base + j])
        own = row(j)
        relacc[rel, :] = relacc[rel, :] + grel[own, :]
        racc[rgt, :] = racc[rgt, :] + gr[own, :]
        nacc[neg, :] = nacc[neg, :] + gn[own, :]

    def gather(j, base):
        own = row(j)
        rvec[own, :] = slab[row(ridx_ref[base + j]), :]
        nvec[own, :] = slab[row(nidx_ref[base + j]), :]

    behind = jnp.maximum(s - 1, 0) * SPAN
    ahead = jnp.minimum(s, spans - 1) * SPAN

    def step(b, carry):
        for u in range(unroll):
            j = b * unroll + u
            gather(j, ahead)
            scatter(j, behind)
        return carry

    lax.fori_loop(0, SPAN // unroll, step, 0)

    @pl.when(s < spans)
    def _():
        hot = (lax.broadcasted_iota(jnp.int32, (ent_ref.shape[0], SPAN), 0) == lhs_ref[0]).astype(F32).astype(BF16)
        eh, el = split(ent_ref[...])
        first = ((0,), (0,))
        last = ((1,), (1,))
        inner = ((1,), (0,))
        left = dot2(hot, eh, first) + dot2(hot, el, first)
        rel = read_rows(rel_ref, SPAN)
        query = left * rel
        live = (s * SPAN + lax.broadcasted_iota(jnp.int32, (SPAN, 1), 0) < cnt_ref[0]).astype(F32)
        q = split(query)
        n = split(read_rows(nvec, SPAN))
        neg = dot3(q, n, last)
        dneg = split(jax.nn.sigmoid(neg) * (live / NEG))
        right = read_rows(rvec, SPAN)
        pos = jnp.sum(query * right, axis=1, keepdims=True)
        dpos = -jax.nn.sigmoid(-pos) * live
        write_rows(gr, dpos * query, SPAN)
        write_rows(gn, dot3(dneg, q, first), SPAN)
        grad_query = dpos * right + dot3(dneg, n, inner)
        write_rows(grel, grad_query * left, SPAN)
        gl = split(grad_query * rel)
        left_ref[...] += dot2(hot, gl[0], inner) + dot2(hot, gl[1], inner)

    @pl.when(s == spans)
    def _():
        def right_member(m, carry):
            for part in range(PARTS):
                for half in range(2):
                    src = pl.multiple_of((m * 256 + part * 64 + half * GROUP) * CHUNKS, 128)
                    out = part_row(m, part) + half * PACK
                    planes = [
                        racc[pl.ds(src + c, GROUP, stride=CHUNKS), :] + nacc[pl.ds(src + c, GROUP, stride=CHUNKS), :]
                        for c in range(CHUNKS)
                    ]
                    for c in range(3):
                        slab[span_of(out + c * GROUP, GROUP), :] = planes[c]
                    slab[span_of(out + 96, 8), :] = pack_tail(planes[3])
            return carry

        lax.fori_loop(0, BLOCKS, right_member, 0)
        out = pltpu.make_async_copy(slab.at[pl.ds(0, right_hbm.shape[0])], right_hbm, sem.at[0])
        out.start()
        begins = (0, 2 * SHARDS * PIECE_ROWS[0], 2 * SHARDS * (PIECE_ROWS[0] + PIECE_ROWS[1]))

        def shards(i, carry):
            for k in range(4):
                group = i * 4 + k
                src = pl.multiple_of(group * GROUP * CHUNKS, 128)
                at = [b + shard_row(group, p, PIECE_SUM) for p, b in enumerate(begins)]
                for c in range(3):
                    nacc[span_of(at[c], GROUP), :] = relacc[pl.ds(src + c, GROUP, stride=CHUNKS), :]
                nacc[span_of(at[2] + GROUP, 8), :] = pack_tail(relacc[pl.ds(src + 3, GROUP, stride=CHUNKS), :])
            return carry

        lax.fori_loop(0, 2 * SHARDS // 4, shards, 0)
        copies = [
            pltpu.make_async_copy(nacc.at[pl.ds(b, ref.shape[0])], ref, sem.at[1 + p])
            for p, (b, ref) in enumerate(zip(begins, (rel0_hbm, rel1_hbm, rel2_hbm)))
        ]
        for copy in copies:
            copy.start()
        for copy in copies:
            copy.wait()
        out.wait()


def bucket(counts, ridx, nidx, rid, lhs, ent, rel_rows, slab):
    edges = rid.shape[0]
    spans = edges // SPAN
    total = slab.shape[0]
    smem = pl.BlockSpec(memory_space=pltpu.SMEM)
    anym = pl.BlockSpec(memory_space=pl.ANY)
    vm = lambda r: pltpu.VMEM((r, LANES), F32)
    span_rows = SPAN * CHUNKS
    return pl.pallas_call(
        functools.partial(bucket_kernel, spans, 8),
        grid=(spans + 1,),
        out_shape=(
            jax.ShapeDtypeStruct((PARTS * BLOCKS * PART, LANES), F32),
            *(jax.ShapeDtypeStruct((2 * SHARDS * r, LANES), F32) for r in PIECE_ROWS),
            jax.ShapeDtypeStruct(ent.shape, F32),
        ),
        in_specs=[
            smem, smem, smem, smem,
            pl.BlockSpec((1, 1, SPAN), lambda s: (jnp.minimum(s, spans - 1), 0, 0)),
            pl.BlockSpec(ent.shape, lambda s: (0, 0)),
            pl.BlockSpec((span_rows, LANES), lambda s: (jnp.minimum(s, spans - 1), 0)),
            anym,
        ],
        out_specs=(anym, anym, anym, anym, pl.BlockSpec(ent.shape, lambda s: (0, 0))),
        scratch_shapes=[
            vm(total + 8), vm(total), vm(total + 8), vm(total),
            vm(span_rows), vm(span_rows), vm(span_rows), vm(span_rows), vm(span_rows),
            pltpu.SemaphoreType.DMA((4,)),
        ],
        compiler_params=pltpu.CompilerParams(vmem_limit_bytes=58 * 2**20),
        name="bucket",
    )(counts, ridx, nidx, rid, lhs, ent, rel_rows, slab)


def ring_rows(half, order):
    size, used = half, 0
    for name in order:
        size = size // (2 if name == "xhi" else RING)
        used += size if name == "xhi" else 3 * size
    return used


def reduce_kernel(
    width,
    state_ref, shard_ref, right_hbm, rel0_hbm, rel1_hbm, rel2_hbm,
    back_hbm, new0_hbm, new1_hbm, new2_hbm,
    *scratch,
):
    racc, rland, rring = scratch[0:4], scratch[4:8], scratch[8:12]
    pacc, pland, pring = scratch[12:15], scratch[15:18], scratch[18:21]
    news = scratch[21:24]
    back, send, recv, local = scratch[24:28]
    at = here()
    greet(
        [toward(at, axis, step) for axis in ("x", "y", "z") for step in (1, -1)]
        + [toward(at, "xhi", 1), toward(at, "core", 1), next_group(1), next_group(-1)]
    )
    net = Copies(send, recv, local)
    region = BLOCKS * PART
    backs = []
    bases = [None] * 3

    def right_flow(part):
        def done(base):
            mine = pl.ds(part * PART, PART)
            copy = net.to(next_group(1), racc[part].at[span_of(base, PART)], back.at[mine])
            yield
            copy.wait_recv()
            backs.append(net.home(back.at[mine], back_hbm.at[mine]))

        return sum_flow(
            net, at, right_hbm.at[pl.ds(part * region, region)], racc[part], rland[part], rring[part],
            PART_ORDER[part], done,
        )

    def piece_flow(piece):
        def done(base):
            bases[piece] = base
            return
            yield

        src = (rel0_hbm, rel1_hbm, rel2_hbm)[piece]
        return sum_flow(net, at, src, pacc[piece], pland[piece], pring[piece], PIECE_SUM[piece], done)

    pieces = [piece_flow(p) for p in range(3)]
    rights = [right_flow(p) for p in range(PARTS)]

    def all_pieces():
        yield from merged(pieces)
        planes = [pacc[p][span_of(bases[p], GROUP), :] for p in range(3)]
        planes.append(unpack_tail(pacc[2][span_of(bases[2] + GROUP, 8), :]))
        squares = planes[0] * planes[0]
        for plane in planes[1:]:
            squares = squares + plane * plane
        state = state_ref[...] + jnp.sum(squares, axis=1, keepdims=True) / width
        root = jnp.sqrt(state)
        fresh = [shard_ref[:, c * LANES : (c + 1) * LANES] - STEP_SIZE * planes[c] / root for c in range(CHUNKS)]
        tail = pack_tail(fresh[3])
        lane = lax.broadcasted_iota(jnp.int32, (8, LANES), 1)
        for g in range(GROUP // 8):
            tail = jnp.where(lane == LANES // 2 + g, state[8 * g : 8 * g + 8], tail)
        outs = (new0_hbm, new1_hbm, new2_hbm)
        flows = []
        for p in range(3):
            mine = (at["core"] * SHARDS + index_of(at, PIECE_OUT[p])) * PIECE_ROWS[p]
            news[p][span_of(mine, GROUP), :] = fresh[p]
            if p == 2:
                news[p][span_of(mine + GROUP, 8), :] = tail

            def arrived(start, size, p=p):
                rows = PIECE_ROWS[p]
                half, k = start // (SHARDS * rows), start // (16 * rows) % RING
                src = news[p].at[span_of(start, size)]
                if p == 0:
                    dst = outs[p].at[half, k]
                    src = src.reshape(4, 4, rows, LANES)
                elif p == 1:
                    dst = outs[p].at[half, :, :, k]
                    src = src.reshape(4, 4, rows, LANES)
                else:
                    dst = outs[p].at[half, :, k]
                    src = src.reshape(4, 4, rows, LANES)
                backs.append(net.home(src, dst))

            flows.append(spread_flow(net, at, news[p], 0, PIECE_ROWS[p], PIECE_OUT[p], arrived))
        yield from merged(flows)

    run_beside(rights, all_pieces())
    for copy in backs:
        copy.wait()
    net.finish()


def reduce(width, state, shard, right, pieces):
    anym = pl.BlockSpec(memory_space=pl.ANY)
    vmem = pl.BlockSpec(memory_space=pltpu.VMEM)
    vm = lambda r: pltpu.VMEM((r, LANES), F32)
    half = BLOCKS // 2 * PART
    return pl.pallas_call(
        functools.partial(reduce_kernel, width),
        out_shape=(
            jax.ShapeDtypeStruct((PARTS * PART, LANES), F32),
            *(jax.ShapeDtypeStruct((2, 4, 4, 4, r, LANES), F32) for r in PIECE_ROWS),
        ),
        in_specs=[vmem, vmem, anym, anym, anym, anym],
        out_specs=(anym,) * 4,
        scratch_shapes=[
            *(vm(half) for _ in range(PARTS)),
            *(vm(half) for _ in range(PARTS)),
            *(vm(ring_rows(half, PART_ORDER[p])) for p in range(PARTS)),
            *(vm(SHARDS * r) for r in PIECE_ROWS),
            *(vm(SHARDS * r) for r in PIECE_ROWS),
            *(vm(ring_rows(SHARDS * r, PIECE_SUM[p])) for p, r in enumerate(PIECE_ROWS)),
            *(vm(2 * SHARDS * r) for r in PIECE_ROWS),
            vm(PARTS * PART),
            pltpu.SemaphoreType.DMA((192,)),
            pltpu.SemaphoreType.DMA((192,)),
            pltpu.SemaphoreType.DMA((64,)),
        ],
        compiler_params=pltpu.CompilerParams(vmem_limit_bytes=56 * 2**20, collective_id=2, has_side_effects=True),
        name="reduce",
    )(state, shard, right, *pieces)


def finish_kernel(width, left_ref, back_ref, ent_ref, state_ref, new0, new1, new2, rel_ref, ent_out, state_out):
    s = pl.program_id(0)
    count = rel_ref.shape[1]
    for k in range(count // LANES):
        out = pl.ds(k * LANES, LANES)
        groups = range(k * 4, k * 4 + 4)
        for c, ref in enumerate((new0, new1, new2)):
            r = PIECE_ROWS[c]
            plane = jnp.concatenate([ref[g * r : g * r + GROUP, :] for g in groups], axis=0)
            rel_ref[c * LANES : (c + 1) * LANES, out] = plane.T
        r = PIECE_ROWS[2]
        tail = jnp.concatenate([unpack_tail(new2[g * r + GROUP : (g + 1) * r, :]) for g in groups], axis=0)
        rel_ref[3 * LANES : width, out] = tail.T[: width - 3 * LANES]

    @pl.when(s == 0)
    def _():
        for j in range(8):
            part = slice(j * GROUP, (j + 1) * GROUP)
            planes = [back_ref[pl.ds(j * PACK + c * GROUP, GROUP), :] for c in range(3)]
            planes.append(unpack_tail(back_ref[pl.ds(j * PACK + 96, 8), :]))
            grad = left_ref[part, :] + jnp.concatenate(planes, axis=1)
            state = state_ref[part, :] + jnp.sum(grad * grad, axis=1, keepdims=True) / width
            state_out[part, :] = state
            fresh = ent_ref[part, :] - STEP_SIZE * grad / jnp.sqrt(state)
            ent_out[part, :] = fresh[:, :width]


def finish(width, left, back, ent, ent_state, news, count):
    steps = 8
    full = lambda a: pl.BlockSpec(a.shape, lambda s: (0, 0))
    rows = ent.shape[0]
    return pl.pallas_call(
        functools.partial(finish_kernel, width),
        grid=(steps,),
        out_shape=(
            jax.ShapeDtypeStruct((width, count), F32),
            jax.ShapeDtypeStruct((rows, width), F32),
            jax.ShapeDtypeStruct((rows, 1), F32),
        ),
        in_specs=[full(a) for a in (left, back, ent, ent_state)]
        + [pl.BlockSpec((2 * SHARDS // steps * r, LANES), lambda s: (s, 0)) for r in PIECE_ROWS],
        out_specs=(
            pl.BlockSpec((width, count // steps), lambda s: (0, s)),
            pl.BlockSpec((rows, width), lambda s: (0, 0)),
            pl.BlockSpec((rows, 1), lambda s: (0, 0)),
        ),
        compiler_params=pltpu.CompilerParams(vmem_limit_bytes=60 * 2**20),
        name="finish",
    )(left, back, ent, ent_state, *news)


def on_device(
    entities, ent_state, relations, rel_state, lhs_rows, rhs_owner, rhs_off, neg_owner, neg_off, rel_ids, counts
):
    shard = entities[0]
    rows, width = shard.shape
    wide = CHUNKS * LANES
    padded = jnp.pad(shard, ((0, 0), (0, wide - width)))
    edges = lhs_rows.shape[1]
    spans = edges // SPAN
    ridx = rhs_owner[0, :, 0] * rows + rhs_off[0]
    nidx = (neg_owner[0, :, 0] * rows + neg_off[0]).reshape(spans, NEG)
    nidx = jnp.pad(nidx, ((0, 0), (0, SPAN - NEG)), constant_values=rows * BLOCKS).reshape(edges)
    rid = rel_ids[0]
    at = here()
    mine = (at["core"] * SHARDS + index_of(at, ("z", "y", "x"))) * GROUP
    rel_shard = jnp.pad(lax.dynamic_slice_in_dim(relations, mine, GROUP, 0), ((0, 0), (0, wide - width)))
    rel_state_shard = lax.dynamic_slice_in_dim(rel_state, mine, GROUP, 0)[:, None]

    slab, rel_rows = fetch(rid, padded, relations.T)
    right, *pieces, left = bucket(counts[0], ridx, nidx, rid, lhs_rows.reshape(spans, 1, SPAN), padded, rel_rows, slab)
    back, *news = reduce(width, rel_state_shard, rel_shard, right, pieces)
    rel_new, new_shard, new_state = finish(
        width, left, back, padded, ent_state[0][:, None], [n.reshape(-1, LANES) for n in news], relations.shape[0]
    )
    states = news[2].reshape(2 * SHARDS, PIECE_ROWS[2], LANES)[:, GROUP:, LANES // 2 : LANES // 2 + 4]
    states = states.transpose(0, 2, 1).reshape(-1)
    return (new_shard[None], new_state.reshape(1, rows), rel_new.T, states)


def solution(mesh):
    in_specs = (
        P("group", "member", None), P("group", "member"), P(), P(),
        P("group", "member"), P("group", "member", None), P("group", "member"),
        P("group", "member", None), P("group", "member"), P("group", "member"), P("group", "member"),
    )
    out_specs = (P("group", "member", None), P("group", "member"), P(), P())
    return jax.shard_map(on_device, mesh=mesh, in_specs=in_specs, out_specs=out_specs, check_vma=False)
```

time: 478 us -> 255 us (0.53)
  waiting for transfers between devices: 307 us -> 0 us
  Pallas kernels: 69.6 us -> 236 us
  local copies, waits for them, and re-layouts: 60.6 us -> 11.6 us
  between operations: 14.6 us -> 1.47 us
  other arithmetic: 17.4 us -> 5.81 us
  starting transfers between devices: 6.95 us -> 0 us
    pallas_call x1 -> x4, Pallas kernels: 69.6 us -> 236 us  [the longest x1 96.8 us: reduce(): pl.pallas_call(functools.partial(reduce_kernel, width), out_shape=(jax.Sh...]
    psum x1 -> x0, waiting for transfers between devices: 159 us -> none  [on_device(): lax.psum(rel_part, ('group', 'member')).reshape(-1, wide)[:, :width]]
    reduce_scatter x1 -> x0, waiting for transfers between devices: 100 us -> none  [on_device(): lax.psum_scatter(right_part, 'member', scatter_dimension=0, tiled=True)]
    all_gather x1 -> x0, waiting for transfers between devices: 33.6 us -> none  [on_device(): slab = lax.all_gather(right, 'member', axis=0, tiled=True)]
    gather x2 -> x0, local copies, waits for them, and re-layouts: 29.3 us -> none  [on_device(): rel_rows = jnp.pad(relations, ((0, 0), (0, wide - width)))[rid]]
    reshape x4 -> x1, local copies, waits for them, and re-layouts: 18.4 us -> 0.86 us  [on_device(): states = states.transpose(0, 2, 1).reshape(-1)]
    ppermute x2 -> x0, waiting for transfers between devices: 13.9 us -> none  [from_behind(): lax.ppermute(array, axis, [(i, (i + by) % devices) for i in range(devices)])]
    sub x1 -> x0, other arithmetic: 9.56 us -> none  [on_device(): relations - STEP_SIZE * rel_total / jnp.sqrt(rel_new_state)[:, None]]
  transfers between devices with their start and end apart: 5 -> 0, of which waited for: 5 -> 0; matrix products, arithmetic and copies ran while one was open for 12% -> 0% of each run, Pallas kernels for 0% -> 0%
where the time goes in v2:
time: 255 us
  Pallas kernels  236 us (93%)
  local copies, waits for them, and re-layouts  11.6 us (5%)
  other arithmetic  5.81 us (2%)
    pallas_call x1, Pallas kernels, reduce(): pl.pallas_call(functools.partial(reduce_kernel, width), out_shape=(jax.Sh...  96.8 us
    pallas_call x1, Pallas kernels, bucket(): pl.pallas_call(functools.partial(bucket_kernel, spans, 8), grid=(spans +...  71.9 us
    pallas_call x1, Pallas kernels, fetch(): pl.pallas_call(fetch_kernel, out_shape=(jax.ShapeDtypeStruct((rows * CHUN...  56.4 us
    pallas_call x1, Pallas kernels, finish(): pl.pallas_call(functools.partial(finish_kernel, width), grid=(steps,), ou...  10.5 us
    unnamed x11, local copies, waits for them, and re-layouts  5.25 us

profile of v2, /device:TPU:1, one launch (start us, length us, event | category | flops | bytes accessed | tf_op | source)
XLA Modules:
  0.0 254.5 jit_solution(11288319988749069618)
XLA Ops:
  1.3 0.7 broadcast_multiply_fusion
  2.0 1.3 add.42.ridx_ref
  3.4 0.8 multiply_reduce_fusion
  4.1 0.1 mul.39
  4.2 0.5 broadcast.24
  4.7 1.4 reduce.9
  6.1 0.1 squeeze.19
  6.3 0.6 copy.27
  6.9 1.2 copy.19
  8.1 0.9 pad.13.ent_ref
  8.9 56.4 %fetch.1 = (f32[16384,128]{1,0:T(8,128)}, f32[16384,128]{1,0:T(8,128)}) custom-call(s32[4096]{0:T(1024)} %bitcast.30, f32[256,512]{1,0:T(8,128)} %pad.13.ent_ref, f32[400,4096]{1,0:T(8,128)} %bitcast.22), custom_call_target="tpu_custom_call" | custom-call | tf_op jit(solution)/shard_map/fetch/pallas_call | solution.py:399
  65.3 71.9 %bucket.1 = (f32[13312,128]{1,0:T(8,128)}, f32[4096,128]{1,0:T(8,128)}, f32[4096,128]{1,0:T(8,128)}, f32[5120,128]{1,0:T(8,128)}, f32[256,512]{1,0:T(8,128)}) custom-call(s32[1]{0:T(128)} %bitcast.21.cnt_ref, s32[4096]{0:T(1024)} %add.42.ridx_ref, s32[4096]{0:T(1024)} %bitcast.32, s32[4096]{0:T(1024)} %bitcast.31, s32[8,1,512]{2,1,0:T(1,128)} %bitcast.34, ...), custom_call_target="tpu_custom_call" | custom-call | tf_op jit(solution)/shard_map/bucket/pallas_call | solution.py:548
  137.4 0.7 copy.21.state_ref
  138.1 1.0 constant_dynamic-slice_fusion
  139.1 0.1 copy.25
  139.2 0.6 pad.14.shard_ref
  139.9 96.8 %reduce.10 = (f32[832,128]{1,0:T(8,128)}, f32[2,4,4,4,32,128]{5,4,3,2,1,0:T(8,128)}, f32[2,4,4,4,32,128]{5,4,3,2,1,0:T(8,128)}, f32[2,4,4,4,40,128]{5,4,3,2,1,0:T(8,128)}) custom-call(f32[32,1]{1,0:T(8,128)} %copy.21.state_ref, f32[32,512]{1,0:T(8,128)} %pad.14.shard_ref, f32[13312,128]{1,0:T(8,128)} %get-tuple-element.21.right_hbm, ...), custom_call_target="tpu_custom_call" | custom-call | tf_op jit(solution)/shard_map/reduce/pallas_call | solution.py:678
  236.7 0.8 copy.22.state_ref
  237.5 10.5 %finish.1 = (f32[400,4096]{1,0:T(8,128)}, f32[256,400]{1,0:T(8,128)}, f32[256,1]{1,0:T(8,128)}) custom-call(f32[256,512]{1,0:T(8,128)} %get-tuple-element.20.left_ref, f32[832,128]{1,0:T(8,128)} %get-tuple-element.25.back_ref, f32[256,512]{1,0:T(8,128)} %pad.13.ent_ref, f32[256,1]{1,0:T(8,128)} %copy.22.state_ref, f32[4096,128]{1,0:T(8,128)} %bitcast.26, ...), custom_call_target="tpu_custom_call" | custom-call | tf_op jit(solution)/shard_map/finish/pallas_call | solution.py:735
  248.0 2.0 copy.24
  250.0 1.6 reduce.3
  251.6 1.2 slice.4
  252.8 0.8 copy.26
  253.7 0.9 reshape.46
  (7 shorter events, 0.1 us)
Async XLA Ops:
  0.6 136.7 %copy-start = (f32[4096]{0:T(1024)S(1)}, f32[4096]{0:T(1024)}, u32[]{:S(2)}) copy-start(f32[4096]{0:T(1024)} %param.14) | copy-start | bytes 49156
  139.9 96.8 %copy-start.1 = (f32[1,256]{1,0:T(1,128)S(1)}, f32[1,256]{1,0:T(1,128)}, u32[]{:S(2)}) copy-start(f32[1,256]{1,0:T(1,128)} %param.12) | copy-start | bytes 3076

commit v3 on v2

--- a/solution.py
+++ b/solution.py
@@ -18,15 +18,22 @@
 TAIL = 16
 GROUP = 32
 PACK = 104
-PARTS = 4
-PART = 208
 BLOCKS = 16
 RING = 4
-PART_ORDER = (("y", "xhi"), ("xhi", "y"), ("y", "xhi"), ("xhi", "y"))
+Y_FIRST = ("y", "xhi")
+X_FIRST = ("xhi", "y")
+PART_IN = (X_FIRST, Y_FIRST) * 2
+PART_SUM = (X_FIRST, Y_FIRST, Y_FIRST, Y_FIRST) * 2
 PIECE_ROWS = (32, 32, 40)
 PIECE_SUM = (("z", "y", "x"), ("x", "z", "y"), ("z", "x", "y"))
 PIECE_OUT = (("z", "y", "x"), ("x", "z", "y"), ("y", "z", "x"))
 SHARDS = 64
+SHIFTS = 8
+RINGS_IN = 8
+RINGS_SUM = 2
+LINK_ROWS = 85.0
+CORE_ROWS = 1000.0
+LATENCY = 1.7
 
 
 def split(x):
@@ -91,10 +98,14 @@
     return at
 
 
-def part_row(member, part):
+def part_size(orders):
+    return 256 // GROUP * PACK // len(orders)
+
+
+def part_row(member, part, orders):
     where = digits_of(member // 2, ("y", "xhi"))
-    at = (member % 2) * 8 + index_of(where, PART_ORDER[part])
-    return part * BLOCKS * PART + at * PART
+    at = (member % 2) * 8 + index_of(where, orders[part])
+    return (part * BLOCKS + at) * part_size(orders)
 
 
 def shard_row(group, piece, orders):
@@ -138,8 +149,9 @@
     def __init__(self, send, recv, local):
         self.send, self.recv, self.local = send, recv, local
         self.started, self.kept, self.homes = 0, [], 0
-
-    def to(self, there, src, dst):
+        self.now, self.busy, self.flows, self.added, self.gates = 0.0, {}, [], 0, {}
+
+    def to(self, there, src, dst, links, rows):
         copy = pltpu.make_async_remote_copy(
             src_ref=src, dst_ref=dst, send_sem=self.send.at[self.started], recv_sem=self.recv.at[self.started],
             device_id=there, device_id_type=MESH,
@@ -147,7 +159,12 @@
         copy.start()
         self.started += 1
         self.kept.append(copy)
-        return copy
+        begin = max([self.now] + [self.busy.get(link, 0.0) for link in links])
+        end = begin + rows / (CORE_ROWS if links == ("core",) else LINK_ROWS)
+        for link in links:
+            self.busy[link] = end
+        self.now += 0.05
+        return copy, end + LATENCY
 
     def home(self, src, dst):
         copy = pltpu.make_async_copy(src, dst, self.local.at[self.homes])
@@ -155,30 +172,51 @@
         self.homes += 1
         return copy
 
+    def enter(self, name, limit):
+        held, waiting = self.gates.setdefault(name, ([], []))
+        if len(held) == limit:
+            yield waiting
+        held.append(None)
+
+    def leave(self, name):
+        held, waiting = self.gates[name]
+        held.pop()
+        if waiting:
+            number, flow = waiting.pop(0)
+            self.step(number, flow)
+
+    def step(self, number, flow):
+        ready = next(flow, None)
+        if ready is None:
+            return
+        if any(ready is waiting for _, waiting in self.gates.values()):
+            ready.append((number, flow))
+        else:
+            self.flows.append((max(r for _, r in ready), number, flow))
+
+    def add(self, flow):
+        self.added += 1
+        self.step(self.added, flow)
+
+    def run(self, beside=iter(()), cost=0.7):
+        while self.flows:
+            entry = min(self.flows)
+            while entry[0] > self.now + cost and next(beside, None) is not None:
+                self.now += cost
+            self.flows.remove(entry)
+            self.now = max(self.now, entry[0]) + 0.1
+            self.step(entry[1], entry[2])
+        for _ in beside:
+            pass
+
     def finish(self):
         for copy in self.kept:
             copy.wait_send()
 
 
-def merged(flows):
-    flows = list(flows)
-    while flows:
-        left = []
-        for flow in flows:
-            try:
-                next(flow)
-            except StopIteration:
-                continue
-            left.append(flow)
-            yield
-        flows = left
-
-
-def run_beside(flows, beside):
-    for _ in merged(flows):
-        next(beside, None)
-    for _ in beside:
-        pass
+def wait_all(copies):
+    for copy, _ in copies:
+        copy.wait_recv()
 
 
 def halves(size):
@@ -202,56 +240,71 @@
     lax.fori_loop(0, size // tile, step, 0)
 
 
-def sum_flow(net, at, src, acc, landing, ring, order, done):
+def both(axis):
+    return (axis + "+", axis + "-")
+
+
+def sum_flow(net, at, src, acc, landing, ring, order, direct, done):
     half = acc.shape[0]
     core = at["core"]
-    over = net.to(toward(at, "core", 1), src.at[span_of((1 - core) * half, half)], landing)
+    over = net.to(toward(at, "core", 1), src.at[span_of((1 - core) * half, half)], landing, ("core",), half)
     own = net.home(src.at[span_of(core * half, half)], acc)
-    yield
+    yield [over]
     own.wait()
-    over.wait_recv()
+    wait_all([over])
     add_into(acc, 0, landing, 0, half)
     base, size, used = 0, half, 0
-    for axis in order:
+    for level, axis in enumerate(order):
         a = at[axis]
         if axis == "xhi":
             size = size // 2
-            copy = net.to(toward(at, axis, 1), acc.at[span_of(base + (1 - a) * size, size)], ring.at[pl.ds(used, size)])
-            yield
-            copy.wait_recv()
+            src_at = acc.at[span_of(base + (1 - a) * size, size)]
+            copies = [net.to(toward(at, axis, 1), src_at, ring.at[pl.ds(used, size)], both("x"), size)]
+            yield copies
+            wait_all(copies)
             add_into(acc, base + a * size, ring, used, size)
             used += size
         else:
             size = size // RING
-            h1, h2 = halves(size)
             up, down, far = (base + (a + k) % RING * size for k in (1, 3, 2))
-            above, below = toward(at, axis, 1), toward(at, axis, -1)
-            ra, rb, rc, rd = used, used + h1, used + size, used + 2 * size
-            first = net.to(above, acc.at[span_of(far, h1)], ring.at[pl.ds(ra, h1)])
-            second = net.to(below, acc.at[span_of(far + h1, h2)], ring.at[pl.ds(rb, h2)])
-            c2 = net.to(above, acc.at[span_of(up + h1, h2)], ring.at[pl.ds(rc + h1, h2)])
-            d1 = net.to(below, acc.at[span_of(down, h1)], ring.at[pl.ds(rd, h1)])
-            yield
-            first.wait_recv()
-            add_into(acc, up, ring, ra, h1)
-            c1 = net.to(above, acc.at[span_of(up, h1)], ring.at[pl.ds(rc, h1)])
-            second.wait_recv()
-            add_into(acc, down + h1, ring, rb, h2)
-            d2 = net.to(below, acc.at[span_of(down + h1, h2)], ring.at[pl.ds(rd + h1, h2)])
-            yield
-            own = base + a * size
-            c2.wait_recv()
-            d1.wait_recv()
-            c1.wait_recv()
-            d2.wait_recv()
-            add_into(acc, own, ring, rc, size)
-            add_into(acc, own, ring, rd, size)
+            above, below, opposite = (toward(at, axis, k) for k in (1, -1, 2))
+            plus, minus = ((link,) for link in both(axis))
+            ra, rc, rd = used, used + size, used + 2 * size
+            if level >= direct:
+                copies = [
+                    net.to(opposite, acc.at[span_of(far, size)], ring.at[pl.ds(ra, size)], both(axis), size),
+                    net.to(above, acc.at[span_of(up, size)], ring.at[pl.ds(rc, size)], plus, size),
+                    net.to(below, acc.at[span_of(down, size)], ring.at[pl.ds(rd, size)], minus, size),
+                ]
+                yield copies
+                wait_all(copies)
+                add_into(acc, base + a * size, ring, ra, size)
+            else:
+                h1, h2 = halves(size)
+                yield from net.enter(axis, RINGS_SUM)
+                first = net.to(above, acc.at[span_of(far, h1)], ring.at[pl.ds(ra, h1)], plus, h1)
+                second = net.to(below, acc.at[span_of(far + h1, h2)], ring.at[pl.ds(ra + h1, h2)], minus, h2)
+                c2 = net.to(above, acc.at[span_of(up + h1, h2)], ring.at[pl.ds(rc + h1, h2)], plus, h2)
+                d1 = net.to(below, acc.at[span_of(down, h1)], ring.at[pl.ds(rd, h1)], minus, h1)
+                yield [first, second]
+                wait_all([first])
+                add_into(acc, up, ring, ra, h1)
+                c1 = net.to(above, acc.at[span_of(up, h1)], ring.at[pl.ds(rc, h1)], plus, h1)
+                wait_all([second])
+                add_into(acc, down + h1, ring, ra + h1, h2)
+                d2 = net.to(below, acc.at[span_of(down + h1, h2)], ring.at[pl.ds(rd + h1, h2)], minus, h2)
+                copies = [c2, d1, c1, d2]
+                yield copies
+                wait_all(copies)
+                net.leave(axis)
+            add_into(acc, base + a * size, ring, rc, size)
+            add_into(acc, base + a * size, ring, rd, size)
             used += 3 * size
         base = base + a * size
     yield from done(base)
 
 
-def spread_flow(net, at, buf, offset, rows, order, arrived):
+def spread_flow(net, at, buf, offset, rows, order, direct, arrived):
     radix = {"xhi": 2, "x": 4, "y": 4, "z": 4}
     total = rows
     for name in order:
@@ -269,48 +322,65 @@
 
     def share(start, size):
         there = span_of(start, size)
-        shared.append((net.to(sibling, buf.at[there], buf.at[there]), start + (1 - 2 * core) * total, size))
-        arrived(start, size)
+        copy = net.to(sibling, buf.at[there], buf.at[there], ("core",), size)
+        shared.append((copy, start + (1 - 2 * core) * total, size))
+
+    def send(there, start, size, links):
+        part = span_of(start, size)
+        return net.to(there, buf.at[part], buf.at[part], links, size)
 
     for level in reversed(range(len(order))):
         name, size, region = order[level], strides[level], bases[level]
         a = at[name]
         last = level == 0
-        own = span_of(region + a * size, size)
         if name == "xhi":
-            copy = net.to(toward(at, name, 1), buf.at[own], buf.at[own])
+            other = region + (1 - a) * size
+            copies = [send(toward(at, name, 1), region + a * size, size, both("x"))]
             if last:
                 share(region + a * size, size)
-            yield
-            copy.wait_recv()
+                arrived(region + a * size, size)
+            yield copies
+            wait_all(copies)
             if last:
-                share(region + (1 - a) * size, size)
+                share(other, size)
+                arrived(other, size)
         else:
             h1, h2 = halves(size)
-            up, down, far = (region + (a + k) % RING * size for k in (1, 3, 2))
-            above, below = toward(at, name, 1), toward(at, name, -1)
-            e = net.to(above, buf.at[own], buf.at[own])
-            f = net.to(below, buf.at[own], buf.at[own])
+            own, up, down, far = (region + (a + k) % RING * size for k in (0, 1, 3, 2))
+            above, below, opposite = (toward(at, name, k) for k in (1, -1, 2))
+            plus, minus = ((link,) for link in both(name))
+            if level < direct:
+                yield from net.enter(name, RINGS_IN)
+            e = send(above, own, size, plus)
+            f = send(below, own, size, minus)
             if last:
-                share(region + a * size, size)
-            yield
-            e.wait_recv()
-            lower = span_of(down, h1)
-            g = net.to(above, buf.at[lower], buf.at[lower])
-            f.wait_recv()
-            upper = span_of(up + h1, h2)
-            h = net.to(below, buf.at[upper], buf.at[upper])
-            if last:
-                share(down, size)
-                share(up, size)
-            yield
-            g.wait_recv()
-            h.wait_recv()
-            if last:
-                share(far, size)
-    yield
+                share(own, size)
+            if level >= direct:
+                g = send(opposite, own, size, both(name))
+                yield [e, f, g]
+                wait_all([e, f, g])
+            else:
+                if last:
+                    arrived(own, size)
+                yield [e, f]
+                wait_all([e])
+                g = send(above, down, h1, plus)
+                wait_all([f])
+                h = send(below, up + h1, h2, minus)
+                if last:
+                    share(down, size)
+                    share(up, size)
+                    arrived(down, size)
+                    arrived(up, size)
+                yield [g, h]
+                wait_all([g, h])
+                net.leave(name)
+                if last:
+                    share(far, size)
+                    arrived(far, size)
     for copy, start, size in shared:
-        copy.wait_recv()
+        yield [copy]
+        wait_all([copy])
         arrived(start, size)
 
 
@@ -329,32 +399,40 @@
         own[pl.ds(j * PACK + 96, 8), :] = pack_tail(ent_ref[rows, 3 * LANES : 4 * LANES])
 
     writes = []
+    parts = len(PART_IN)
+    size = part_size(PART_IN)
+    groups = size // PACK
 
     def flow(part):
-        start = part * BLOCKS * PART
-        mine = span_of(part_row(m, part), PART)
-        shift = net.to(next_group(-1), own.at[pl.ds(part * PART, PART)], packed.at[mine])
-        yield
-        shift.wait_recv()
-
-        def arrived(begin, size):
+        start = part * BLOCKS * size
+        mine = span_of(part_row(m, part, PART_IN), size)
+        yield from net.enter("shift", SHIFTS)
+        shift = net.to(next_group(-1), own.at[pl.ds(part * size, size)], packed.at[mine], ("z-",), size)
+        yield [shift]
+        wait_all([shift])
+        net.leave("shift")
+
+        def arrived(begin, rows):
             def block(i, carry):
-                source = begin + i * PART
-                flat = (source - start) // PART
-                where = digits_of(flat % 8, PART_ORDER[part])
+                source = begin + i * size
+                flat = (source - start) // size
+                where = digits_of(flat % 8, PART_IN[part])
                 member = (where["y"] * 2 + where["xhi"]) * 2 + flat // 8
-                for half in range(2):
-                    base = source + half * PACK
-                    out = (member * 256 + part * 64 + half * GROUP) * CHUNKS
+                for k in range(groups):
+                    base = source + k * PACK
+                    out = (member * 256 + (part * groups + k) * GROUP) * CHUNKS
                     out = pl.multiple_of(out, 128)
                     for c in range(3):
                         slab[pl.ds(out + c, GROUP, stride=CHUNKS), :] = packed[span_of(base + c * GROUP, GROUP), :]
                     slab[pl.ds(out + 3, GROUP, stride=CHUNKS), :] = unpack_tail(packed[span_of(base + 96, 8), :])
                 return carry
 
-            lax.fori_loop(0, size // PART, block, 0)
-
-        yield from spread_flow(net, at, packed, start, PART, PART_ORDER[part], arrived)
+            lax.fori_loop(0, rows // size, block, 0)
+            net.now += 0.04 * rows / PACK
+
+        yield from spread_flow(net, at, packed, start, size, PART_IN[part], 9, arrived)
+        view = (BLOCKS, parts, groups * GROUP * CHUNKS, LANES)
+        writes.append(net.home(slab.reshape(view).at[:, part], slab_hbm.reshape(view).at[:, part]))
 
     def gather():
         tile = 256
@@ -369,7 +447,7 @@
                 return carry
 
             lax.fori_loop(0, 4, convert, 0)
-            yield
+            yield True
         edges = got.shape[0] // CHUNKS
         segment, unroll = 512, 16
         for t in range(edges // segment):
@@ -382,10 +460,11 @@
             lax.fori_loop(0, segment // unroll, step, 0)
             part = pl.ds(t * segment * CHUNKS, segment * CHUNKS)
             writes.append(net.home(got.at[part], rows_hbm.at[part]))
-            yield
-
-    run_beside([flow(part) for part in range(PARTS)], gather())
-    writes.append(net.home(slab, slab_hbm))
+            yield True
+
+    for part in range(parts):
+        net.add(flow(part))
+    net.run(gather())
     for write in writes:
         write.wait()
     net.finish()
@@ -405,15 +484,15 @@
         in_specs=[pl.BlockSpec(memory_space=pltpu.SMEM), pl.BlockSpec(memory_space=pltpu.VMEM), anym],
         out_specs=(anym, anym),
         scratch_shapes=[
-            pltpu.VMEM((PARTS * PART, LANES), F32),
-            pltpu.VMEM((PARTS * BLOCKS * PART, LANES), F32),
+            pltpu.VMEM((256 // GROUP * PACK, LANES), F32),
+            pltpu.VMEM((rows // GROUP * PACK, LANES), F32),
             pltpu.VMEM((rows * CHUNKS, LANES), F32),
             pltpu.VMEM((width, count), F32),
             pltpu.VMEM((count, CHUNKS, LANES), F32),
             pltpu.VMEM((edges * CHUNKS, LANES), F32),
-            pltpu.SemaphoreType.DMA((96,)),
-            pltpu.SemaphoreType.DMA((96,)),
-            pltpu.SemaphoreType.DMA((16,)),
+            pltpu.SemaphoreType.DMA((128,)),
+            pltpu.SemaphoreType.DMA((128,)),
+            pltpu.SemaphoreType.DMA((24,)),
         ],
         compiler_params=pltpu.CompilerParams(vmem_limit_bytes=56 * 2**20, collective_id=1, has_side_effects=True),
         name="fetch",
@@ -438,9 +517,6 @@
         nacc[...] = jnp.zeros_like(nacc)
         relacc[...] = jnp.zeros_like(relacc)
         left_ref[...] = jnp.zeros_like(left_ref)
-        gr[...] = jnp.zeros_like(gr)
-        gn[...] = jnp.zeros_like(gn)
-        grel[...] = jnp.zeros_like(grel)
         load.wait()
 
     def scatter(j, base):
@@ -457,17 +533,29 @@
         rvec[own, :] = slab[row(ridx_ref[base + j]), :]
         nvec[own, :] = slab[row(nidx_ref[base + j]), :]
 
-    behind = jnp.maximum(s - 1, 0) * SPAN
-    ahead = jnp.minimum(s, spans - 1) * SPAN
-
-    def step(b, carry):
-        for u in range(unroll):
-            j = b * unroll + u
-            gather(j, ahead)
-            scatter(j, behind)
-        return carry
-
-    lax.fori_loop(0, SPAN // unroll, step, 0)
+    behind = (s - 1) * SPAN
+    ahead = s * SPAN
+
+    def rows_loop(*works):
+        def step(b, carry):
+            for u in range(unroll):
+                for work, base in works:
+                    work(b * unroll + u, base)
+            return carry
+
+        lax.fori_loop(0, SPAN // unroll, step, 0)
+
+    @pl.when(s == 0)
+    def _():
+        rows_loop((gather, ahead))
+
+    @pl.when((s > 0) & (s < spans))
+    def _():
+        rows_loop((gather, ahead), (scatter, behind))
+
+    @pl.when(s == spans)
+    def _():
+        rows_loop((scatter, behind))
 
     @pl.when(s < spans)
     def _():
@@ -497,10 +585,11 @@
     @pl.when(s == spans)
     def _():
         def right_member(m, carry):
-            for part in range(PARTS):
-                for half in range(2):
-                    src = pl.multiple_of((m * 256 + part * 64 + half * GROUP) * CHUNKS, 128)
-                    out = part_row(m, part) + half * PACK
+            for part in range(len(PART_SUM)):
+                for k in range(256 // GROUP // len(PART_SUM)):
+                    at = part * (256 // GROUP // len(PART_SUM)) + k
+                    src = pl.multiple_of((m * 256 + at * GROUP) * CHUNKS, 128)
+                    out = part_row(m, part, PART_SUM) + k * PACK
                     planes = [
                         racc[pl.ds(src + c, GROUP, stride=CHUNKS), :] + nacc[pl.ds(src + c, GROUP, stride=CHUNKS), :]
                         for c in range(CHUNKS)
@@ -546,10 +635,10 @@
     vm = lambda r: pltpu.VMEM((r, LANES), F32)
     span_rows = SPAN * CHUNKS
     return pl.pallas_call(
-        functools.partial(bucket_kernel, spans, 8),
+        functools.partial(bucket_kernel, spans, 16),
         grid=(spans + 1,),
         out_shape=(
-            jax.ShapeDtypeStruct((PARTS * BLOCKS * PART, LANES), F32),
+            jax.ShapeDtypeStruct((BLOCKS * 256 // GROUP * PACK, LANES), F32),
             *(jax.ShapeDtypeStruct((2 * SHARDS * r, LANES), F32) for r in PIECE_ROWS),
             jax.ShapeDtypeStruct(ent.shape, F32),
         ),
@@ -585,47 +674,48 @@
     back_hbm, new0_hbm, new1_hbm, new2_hbm,
     *scratch,
 ):
-    racc, rland, rring = scratch[0:4], scratch[4:8], scratch[8:12]
-    pacc, pland, pring = scratch[12:15], scratch[15:18], scratch[18:21]
-    news = scratch[21:24]
-    back, send, recv, local = scratch[24:28]
+    scratch = list(scratch)
+    take = lambda n: [scratch.pop(0) for _ in range(n)]
+    parts = len(PART_SUM)
+    racc, rland, rring = take(parts), take(parts), take(parts)
+    pacc, pland, pring, news = take(3), take(3), take(3), take(3)
+    back, send, recv, local = scratch
     at = here()
     greet(
-        [toward(at, axis, step) for axis in ("x", "y", "z") for step in (1, -1)]
-        + [toward(at, "xhi", 1), toward(at, "core", 1), next_group(1), next_group(-1)]
+        [toward(at, axis, step) for axis in ("x", "y", "z") for step in (1, -1, 2)]
+        + [toward(at, "core", 1), next_group(1), next_group(-1)]
     )
     net = Copies(send, recv, local)
-    region = BLOCKS * PART
+    size = part_size(PART_SUM)
+    region = BLOCKS * size
     backs = []
-    bases = [None] * 3
+    bases = {}
 
     def right_flow(part):
         def done(base):
-            mine = pl.ds(part * PART, PART)
-            copy = net.to(next_group(1), racc[part].at[span_of(base, PART)], back.at[mine])
-            yield
-            copy.wait_recv()
+            mine = pl.ds(part * size, size)
+            src = racc[part].at[span_of(base, size)]
+            copies = [net.to(next_group(1), src, back.at[mine], ("z+",), size)]
+            yield copies
+            wait_all(copies)
             backs.append(net.home(back.at[mine], back_hbm.at[mine]))
 
         return sum_flow(
             net, at, right_hbm.at[pl.ds(part * region, region)], racc[part], rland[part], rring[part],
-            PART_ORDER[part], done,
+            PART_SUM[part], 9, done,
         )
 
     def piece_flow(piece):
         def done(base):
             bases[piece] = base
-            return
-            yield
+            if len(bases) == 3:
+                update()
+            yield from ()
 
         src = (rel0_hbm, rel1_hbm, rel2_hbm)[piece]
-        return sum_flow(net, at, src, pacc[piece], pland[piece], pring[piece], PIECE_SUM[piece], done)
-
-    pieces = [piece_flow(p) for p in range(3)]
-    rights = [right_flow(p) for p in range(PARTS)]
-
-    def all_pieces():
-        yield from merged(pieces)
+        return sum_flow(net, at, src, pacc[piece], pland[piece], pring[piece], PIECE_SUM[piece], 1, done)
+
+    def update():
         planes = [pacc[p][span_of(bases[p], GROUP), :] for p in range(3)]
         planes.append(unpack_tail(pacc[2][span_of(bases[2] + GROUP, 8), :]))
         squares = planes[0] * planes[0]
@@ -639,7 +729,7 @@
         for g in range(GROUP // 8):
             tail = jnp.where(lane == LANES // 2 + g, state[8 * g : 8 * g + 8], tail)
         outs = (new0_hbm, new1_hbm, new2_hbm)
-        flows = []
+        net.now += 0.5
         for p in range(3):
             mine = (at["core"] * SHARDS + index_of(at, PIECE_OUT[p])) * PIECE_ROWS[p]
             news[p][span_of(mine, GROUP), :] = fresh[p]
@@ -649,22 +739,18 @@
             def arrived(start, size, p=p):
                 rows = PIECE_ROWS[p]
                 half, k = start // (SHARDS * rows), start // (16 * rows) % RING
-                src = news[p].at[span_of(start, size)]
-                if p == 0:
-                    dst = outs[p].at[half, k]
-                    src = src.reshape(4, 4, rows, LANES)
-                elif p == 1:
-                    dst = outs[p].at[half, :, :, k]
-                    src = src.reshape(4, 4, rows, LANES)
-                else:
-                    dst = outs[p].at[half, :, k]
-                    src = src.reshape(4, 4, rows, LANES)
+                src = news[p].at[span_of(start, size)].reshape(4, 4, rows, LANES)
+                dst = (outs[p].at[half, k], outs[p].at[half, :, :, k], outs[p].at[half, :, k])[p]
                 backs.append(net.home(src, dst))
 
-            flows.append(spread_flow(net, at, news[p], 0, PIECE_ROWS[p], PIECE_OUT[p], arrived))
-        yield from merged(flows)
-
-    run_beside(rights, all_pieces())
+            net.add(spread_flow(net, at, news[p], 0, PIECE_ROWS[p], PIECE_OUT[p], 1, arrived))
+
+    for k in range(max(3, parts)):
+        if k < 3:
+            net.add(piece_flow(k))
+        if k < parts:
+            net.add(right_flow(k))
+    net.run()
     for copy in backs:
         copy.wait()
     net.finish()
@@ -674,24 +760,25 @@
     anym = pl.BlockSpec(memory_space=pl.ANY)
     vmem = pl.BlockSpec(memory_space=pltpu.VMEM)
     vm = lambda r: pltpu.VMEM((r, LANES), F32)
-    half = BLOCKS // 2 * PART
+    parts = len(PART_SUM)
+    half = BLOCKS // 2 * part_size(PART_SUM)
     return pl.pallas_call(
         functools.partial(reduce_kernel, width),
         out_shape=(
-            jax.ShapeDtypeStruct((PARTS * PART, LANES), F32),
+            jax.ShapeDtypeStruct((256 // GROUP * PACK, LANES), F32),
             *(jax.ShapeDtypeStruct((2, 4, 4, 4, r, LANES), F32) for r in PIECE_ROWS),
         ),
         in_specs=[vmem, vmem, anym, anym, anym, anym],
         out_specs=(anym,) * 4,
         scratch_shapes=[
-            *(vm(half) for _ in range(PARTS)),
-            *(vm(half) for _ in range(PARTS)),
-            *(vm(ring_rows(half, PART_ORDER[p])) for p in range(PARTS)),
+            *(vm(half) for _ in range(parts)),
+            *(vm(half) for _ in range(parts)),
+            *(vm(ring_rows(half, PART_SUM[p])) for p in range(parts)),
             *(vm(SHARDS * r) for r in PIECE_ROWS),
             *(vm(SHARDS * r) for r in PIECE_ROWS),
             *(vm(ring_rows(SHARDS * r, PIECE_SUM[p])) for p, r in enumerate(PIECE_ROWS)),
             *(vm(2 * SHARDS * r) for r in PIECE_ROWS),
-            vm(PARTS * PART),
+            vm(256 // GROUP * PACK),
             pltpu.SemaphoreType.DMA((192,)),
             pltpu.SemaphoreType.DMA((192,)),
             pltpu.SemaphoreType.DMA((64,)),
@@ -701,9 +788,12 @@
     )(state, shard, right, *pieces)
 
 
-def finish_kernel(width, left_ref, back_ref, ent_ref, state_ref, new0, new1, new2, rel_ref, ent_out, state_out):
+def finish_kernel(
+    width, left_ref, back_ref, ent_ref, state_ref, new0, new1, new2, rel_ref, rel_state_ref, ent_out, state_out
+):
     s = pl.program_id(0)
     count = rel_ref.shape[1]
+    lane = lax.broadcasted_iota(jnp.int32, (8, LANES), 1)
     for k in range(count // LANES):
         out = pl.ds(k * LANES, LANES)
         groups = range(k * 4, k * 4 + 4)
@@ -712,40 +802,52 @@
             plane = jnp.concatenate([ref[g * r : g * r + GROUP, :] for g in groups], axis=0)
             rel_ref[c * LANES : (c + 1) * LANES, out] = plane.T
         r = PIECE_ROWS[2]
-        tail = jnp.concatenate([unpack_tail(new2[g * r + GROUP : (g + 1) * r, :]) for g in groups], axis=0)
-        rel_ref[3 * LANES : width, out] = tail.T[: width - 3 * LANES]
+        tails = []
+        for group in groups:
+            packed = new2[group * r + GROUP : (group + 1) * r, :]
+            for g in range(GROUP // 8):
+                state = pltpu.roll(packed, LANES // 2 + TAIL - g, 1)
+                values = packed if g == 0 else pltpu.roll(packed, LANES - TAIL * g, 1)
+                tails.append(jnp.where(lane < TAIL, values, state))
+        tail = jnp.concatenate(tails, axis=0).T
+        rel_ref[3 * LANES : width, out] = tail[: width - 3 * LANES]
+        rel_state_ref[:, out] = tail[TAIL : TAIL + 1]
 
     @pl.when(s == 0)
     def _():
-        for j in range(8):
-            part = slice(j * GROUP, (j + 1) * GROUP)
-            planes = [back_ref[pl.ds(j * PACK + c * GROUP, GROUP), :] for c in range(3)]
-            planes.append(unpack_tail(back_ref[pl.ds(j * PACK + 96, 8), :]))
-            grad = left_ref[part, :] + jnp.concatenate(planes, axis=1)
-            state = state_ref[part, :] + jnp.sum(grad * grad, axis=1, keepdims=True) / width
-            state_out[part, :] = state
-            fresh = ent_ref[part, :] - STEP_SIZE * grad / jnp.sqrt(state)
-            ent_out[part, :] = fresh[:, :width]
+        for i in range(2):
+            part = slice(i * LANES, (i + 1) * LANES)
+            wide = []
+            for j in range(4 * i, 4 * i + 4):
+                planes = [back_ref[pl.ds(j * PACK + c * GROUP, GROUP), :] for c in range(3)]
+                planes.append(unpack_tail(back_ref[pl.ds(j * PACK + 96, 8), :]))
+                wide.append(jnp.concatenate(planes, axis=1))
+            grad = (left_ref[part, :] + jnp.concatenate(wide, axis=0)).T[:width]
+            state = state_ref[:, part] + jnp.sum(grad * grad, axis=0, keepdims=True) / width
+            state_out[:, part] = state
+            ent_out[:, part] = ent_ref[:, part] - STEP_SIZE * grad / jnp.sqrt(state)
 
 
 def finish(width, left, back, ent, ent_state, news, count):
     steps = 8
     full = lambda a: pl.BlockSpec(a.shape, lambda s: (0, 0))
-    rows = ent.shape[0]
+    rows = ent.shape[1]
     return pl.pallas_call(
         functools.partial(finish_kernel, width),
         grid=(steps,),
         out_shape=(
             jax.ShapeDtypeStruct((width, count), F32),
-            jax.ShapeDtypeStruct((rows, width), F32),
-            jax.ShapeDtypeStruct((rows, 1), F32),
+            jax.ShapeDtypeStruct((1, count), F32),
+            jax.ShapeDtypeStruct((width, rows), F32),
+            jax.ShapeDtypeStruct((1, rows), F32),
         ),
         in_specs=[full(a) for a in (left, back, ent, ent_state)]
         + [pl.BlockSpec((2 * SHARDS // steps * r, LANES), lambda s: (s, 0)) for r in PIECE_ROWS],
         out_specs=(
             pl.BlockSpec((width, count // steps), lambda s: (0, s)),
-            pl.BlockSpec((rows, width), lambda s: (0, 0)),
-            pl.BlockSpec((rows, 1), lambda s: (0, 0)),
+            pl.BlockSpec((1, count // steps), lambda s: (0, s)),
+            pl.BlockSpec((width, rows), lambda s: (0, 0)),
+            pl.BlockSpec((1, rows), lambda s: (0, 0)),
         ),
         compiler_params=pltpu.CompilerParams(vmem_limit_bytes=60 * 2**20),
         name="finish",
@@ -773,12 +875,10 @@
     slab, rel_rows = fetch(rid, padded, relations.T)
     right, *pieces, left = bucket(counts[0], ridx, nidx, rid, lhs_rows.reshape(spans, 1, SPAN), padded, rel_rows, slab)
     back, *news = reduce(width, rel_state_shard, rel_shard, right, pieces)
-    rel_new, new_shard, new_state = finish(
-        width, left, back, padded, ent_state[0][:, None], [n.reshape(-1, LANES) for n in news], relations.shape[0]
+    rel_new, states, new_shard, new_state = finish(
+        width, left, back, shard.T, ent_state, [n.reshape(-1, LANES) for n in news], relations.shape[0]
     )
-    states = news[2].reshape(2 * SHARDS, PIECE_ROWS[2], LANES)[:, GROUP:, LANES // 2 : LANES // 2 + 4]
-    states = states.transpose(0, 2, 1).reshape(-1)
-    return (new_shard[None], new_state.reshape(1, rows), rel_new.T, states)
+    return (new_shard.T[None], new_state, rel_new.T, states.reshape(-1))
 
 
 def solution(mesh):

time: 255 us -> 216 us (0.85)
  Pallas kernels: 236 us -> 204 us
  local copies, waits for them, and re-layouts: 11.6 us -> 5.88 us
    pallas_call x1, Pallas kernels: 96.8 us -> 74.9 us  [reduce(): pl.pallas_call(functools.partial(reduce_kernel, width), out_shape=(jax.Sh...]
    pallas_call x1, Pallas kernels: 56.4 us -> 50.1 us  [fetch(): pl.pallas_call(fetch_kernel, out_shape=(jax.ShapeDtypeStruct((rows * CHUN...]
    pallas_call x1, Pallas kernels: 71.9 us -> 68 us  [bucket(): pl.pallas_call(functools.partial(bucket_kernel, spans, 16), grid=(spans +...]
    unnamed x11 -> x7, local copies, waits for them, and re-layouts: 5.25 us -> 2.44 us
where the time goes in v3:
time: 216 us; the launch traced here: 215 us
  Pallas kernels  204 us (94%)
  local copies, waits for them, and re-layouts  5.88 us (3%)
  other arithmetic  4.23 us (2%)
    pallas_call x1, Pallas kernels, reduce(): pl.pallas_call(functools.partial(reduce_kernel, width), out_shape=(jax.Sh...  74.9 us
    pallas_call x1, Pallas kernels, bucket(): pl.pallas_call(functools.partial(bucket_kernel, spans, 16), grid=(spans +...  68 us
    pallas_call x1, Pallas kernels, fetch(): pl.pallas_call(fetch_kernel, out_shape=(jax.ShapeDtypeStruct((rows * CHUN...  50.1 us
    pallas_call x1, Pallas kernels, finish(): pl.pallas_call(functools.partial(finish_kernel, width), grid=(steps,), ou...  10.7 us

profile of v3, /device:TPU:1, one launch (start us, length us, event | category | flops | bytes accessed | tf_op | source)
XLA Modules:
  0.0 215.2 jit_solution(16799810861811751330)
XLA Ops:
  0.6 0.0 copy-start
  1.3 0.7 broadcast_multiply_fusion
  2.0 1.3 add.42.ridx_ref
  3.4 0.8 multiply_reduce_fusion
  4.1 0.1 mul.39
  4.2 0.5 broadcast.23
  4.7 1.4 reduce.8
  6.1 0.1 squeeze.19
  6.3 0.6 copy.21
  6.9 1.2 copy.20
  8.1 0.8 pad.13.clone.ent_ref
  8.9 50.1 %fetch.1 = (f32[16384,128]{1,0:T(8,128)}, f32[16384,128]{1,0:T(8,128)}) custom-call(s32[4096]{0:T(1024)} %bitcast.29, f32[256,512]{1,0:T(8,128)} %pad.13.clone.ent_ref, f32[400,4096]{1,0:T(8,128)} %bitcast.23), custom_call_target="tpu_custom_call" | custom-call | tf_op jit(solution)/shard_map/fetch/pallas_call | solution.py:478
  59.0 68.0 %bucket.1 = (f32[13312,128]{1,0:T(8,128)}, f32[4096,128]{1,0:T(8,128)}, f32[4096,128]{1,0:T(8,128)}, f32[5120,128]{1,0:T(8,128)}, f32[256,512]{1,0:T(8,128)}) custom-call(s32[1]{0:T(128)} %bitcast.22.cnt_ref, s32[4096]{0:T(1024)} %add.42.ridx_ref, s32[4096]{0:T(1024)} %bitcast.31, s32[4096]{0:T(1024)} %bitcast.30, s32[8,1,512]{2,1,0:T(1,128)} %bitcast.33, ...), custom_call_target="tpu_custom_call" | custom-call | tf_op jit(solution)/shard_map/bucket/pallas_call | solution.py:637
  127.1 0.0 copy-done
  127.1 0.1 dynamic-slice_bitcast_fusion
  127.2 0.7 copy.18.state_ref
  127.9 1.0 constant_dynamic-slice_fusion
  128.9 0.1 copy.19
  129.0 0.6 pad.14.shard_ref
  129.6 74.9 %reduce.9 = (f32[832,128]{1,0:T(8,128)}, f32[2,4,4,4,32,128]{5,4,3,2,1,0:T(8,128)}, f32[2,4,4,4,32,128]{5,4,3,2,1,0:T(8,128)}, f32[2,4,4,4,40,128]{5,4,3,2,1,0:T(8,128)}) custom-call(f32[32,1]{1,0:T(8,128)} %copy.18.state_ref, f32[32,512]{1,0:T(8,128)} %pad.14.shard_ref, f32[13312,128]{1,0:T(8,128)} %get-tuple-element.22.right_hbm, ...), custom_call_target="tpu_custom_call" | custom-call | tf_op jit(solution)/shard_map/reduce/pallas_call | solution.py:765
  204.5 10.7 %finish.1 = (f32[400,4096]{1,0:T(8,128)}, f32[1,4096]{1,0:T(1,128)}, f32[400,256]{1,0:T(8,128)}, f32[1,256]{1,0:T(1,128)}) custom-call(f32[256,512]{1,0:T(8,128)} %get-tuple-element.21.left_ref, f32[832,128]{1,0:T(8,128)} %get-tuple-element.26.back_ref, f32[400,256]{1,0:T(8,128)} %bitcast.28, f32[1,256]{1,0:T(1,128)} %state_ref.1, f32[4096,128]{1,0:T(8,128)} %bitcast.25, ...), custom_call_target="tpu_custom_call" | custom-call | tf_op jit(solution)/shard_map/finish/pallas_call | solution.py:835
  (2 shorter events, 0.0 us)
Async XLA Ops:
  0.6 126.4 %copy-start = (f32[4096]{0:T(1024)S(1)}, f32[4096]{0:T(1024)}, u32[]{:S(2)}) copy-start(f32[4096]{0:T(1024)} %param.14) | copy-start | bytes 49156

commit v4 on v3

--- a/solution.py
+++ b/solution.py
@@ -22,7 +22,7 @@
 RING = 4
 Y_FIRST = ("y", "xhi")
 X_FIRST = ("xhi", "y")
-PART_IN = (X_FIRST, Y_FIRST) * 2
+PART_IN = (X_FIRST, Y_FIRST) * 3 + (Y_FIRST, Y_FIRST)
 PART_SUM = (X_FIRST, Y_FIRST, Y_FIRST, Y_FIRST) * 2
 PIECE_ROWS = (32, 32, 40)
 PIECE_SUM = (("z", "y", "x"), ("x", "z", "y"), ("z", "x", "y"))
@@ -31,9 +31,9 @@
 SHIFTS = 8
 RINGS_IN = 8
 RINGS_SUM = 2
-LINK_ROWS = 85.0
+LINK_ROWS = 70.0
 CORE_ROWS = 1000.0
-LATENCY = 1.7
+LATENCY = 4.0
 
 
 def split(x):
@@ -46,9 +46,9 @@
 
 
 def dot3(a, b, dims):
-    ah, al = a
-    bh, bl = b
-    return dot2(ah, bh, dims) + (dot2(ah, bl, dims) + dot2(al, bh, dims))
+    (ah, al), (bh, bl) = a, b
+    (ka,), (kb,) = dims
+    return dot2(jnp.concatenate([ah, ah, al], axis=ka), jnp.concatenate([bh, bl, bh], axis=kb), dims)
 
 
 def row(i):
@@ -564,7 +564,7 @@
         first = ((0,), (0,))
         last = ((1,), (1,))
         inner = ((1,), (0,))
-        left = dot2(hot, eh, first) + dot2(hot, el, first)
+        left = dot2(jnp.concatenate([hot, hot], axis=0), jnp.concatenate([eh, el], axis=0), first)
         rel = read_rows(rel_ref, SPAN)
         query = left * rel
         live = (s * SPAN + lax.broadcasted_iota(jnp.int32, (SPAN, 1), 0) < cnt_ref[0]).astype(F32)
@@ -579,8 +579,8 @@
         write_rows(gn, dot3(dneg, q, first), SPAN)
         grad_query = dpos * right + dot3(dneg, n, inner)
         write_rows(grel, grad_query * left, SPAN)
-        gl = split(grad_query * rel)
-        left_ref[...] += dot2(hot, gl[0], inner) + dot2(hot, gl[1], inner)
+        gl = jnp.concatenate(split(grad_query * rel), axis=0)
+        left_ref[...] += dot2(jnp.concatenate([hot, hot], axis=1), gl, inner)
 
     @pl.when(s == spans)
     def _():
@@ -670,7 +670,7 @@
 
 def reduce_kernel(
     width,
-    state_ref, shard_ref, right_hbm, rel0_hbm, rel1_hbm, rel2_hbm,
+    states_ref, rel_hbm, right_hbm, rel0_hbm, rel1_hbm, rel2_hbm,
     back_hbm, new0_hbm, new1_hbm, new2_hbm,
     *scratch,
 ):
@@ -679,13 +679,17 @@
     parts = len(PART_SUM)
     racc, rland, rring = take(parts), take(parts), take(parts)
     pacc, pland, pring, news = take(3), take(3), take(3), take(3)
-    back, send, recv, local = scratch
+    back, block, shard, send, recv, local = scratch
     at = here()
+    mine = (at["core"] * SHARDS + index_of(at, ("z", "y", "x"))) * GROUP
+    inside = pl.ds(pl.multiple_of(mine % LANES, GROUP), GROUP)
+    lanes = pl.ds(pl.multiple_of(mine // LANES * LANES, LANES), LANES)
     greet(
         [toward(at, axis, step) for axis in ("x", "y", "z") for step in (1, -1, 2)]
         + [toward(at, "core", 1), next_group(1), next_group(-1)]
     )
     net = Copies(send, recv, local)
+    entry = net.home(rel_hbm.at[:, lanes], block)
     size = part_size(PART_SUM)
     region = BLOCKS * size
     backs = []
@@ -721,9 +725,15 @@
         squares = planes[0] * planes[0]
         for plane in planes[1:]:
             squares = squares + plane * plane
-        state = state_ref[...] + jnp.sum(squares, axis=1, keepdims=True) / width
+        entry.wait()
+        height = CHUNKS * LANES
+        wide = jnp.concatenate([block[...], jnp.zeros((height - width, LANES), F32)], axis=0)
+        old = jnp.broadcast_to(states_ref[:, lanes], (LANES, LANES)).T
+        shard[:, 0:height] = wide.T
+        shard[:, height : height + LANES] = old
+        state = shard[inside, height : height + 1] + jnp.sum(squares, axis=1, keepdims=True) / width
         root = jnp.sqrt(state)
-        fresh = [shard_ref[:, c * LANES : (c + 1) * LANES] - STEP_SIZE * planes[c] / root for c in range(CHUNKS)]
+        fresh = [shard[inside, c * LANES : (c + 1) * LANES] - STEP_SIZE * planes[c] / root for c in range(CHUNKS)]
         tail = pack_tail(fresh[3])
         lane = lax.broadcasted_iota(jnp.int32, (8, LANES), 1)
         for g in range(GROUP // 8):
@@ -731,10 +741,10 @@
         outs = (new0_hbm, new1_hbm, new2_hbm)
         net.now += 0.5
         for p in range(3):
-            mine = (at["core"] * SHARDS + index_of(at, PIECE_OUT[p])) * PIECE_ROWS[p]
-            news[p][span_of(mine, GROUP), :] = fresh[p]
+            place = (at["core"] * SHARDS + index_of(at, PIECE_OUT[p])) * PIECE_ROWS[p]
+            news[p][span_of(place, GROUP), :] = fresh[p]
             if p == 2:
-                news[p][span_of(mine + GROUP, 8), :] = tail
+                news[p][span_of(place + GROUP, 8), :] = tail
 
             def arrived(start, size, p=p):
                 rows = PIECE_ROWS[p]
@@ -756,7 +766,7 @@
     net.finish()
 
 
-def reduce(width, state, shard, right, pieces):
+def reduce(width, states, relations, right, pieces):
     anym = pl.BlockSpec(memory_space=pl.ANY)
     vmem = pl.BlockSpec(memory_space=pltpu.VMEM)
     vm = lambda r: pltpu.VMEM((r, LANES), F32)
@@ -768,7 +778,7 @@
             jax.ShapeDtypeStruct((256 // GROUP * PACK, LANES), F32),
             *(jax.ShapeDtypeStruct((2, 4, 4, 4, r, LANES), F32) for r in PIECE_ROWS),
         ),
-        in_specs=[vmem, vmem, anym, anym, anym, anym],
+        in_specs=[vmem, anym, anym, anym, anym, anym],
         out_specs=(anym,) * 4,
         scratch_shapes=[
             *(vm(half) for _ in range(parts)),
@@ -779,13 +789,15 @@
             *(vm(ring_rows(SHARDS * r, PIECE_SUM[p])) for p, r in enumerate(PIECE_ROWS)),
             *(vm(2 * SHARDS * r) for r in PIECE_ROWS),
             vm(256 // GROUP * PACK),
+            pltpu.VMEM((width, LANES), F32),
+            pltpu.VMEM((LANES, (CHUNKS + 1) * LANES), F32),
             pltpu.SemaphoreType.DMA((192,)),
             pltpu.SemaphoreType.DMA((192,)),
             pltpu.SemaphoreType.DMA((64,)),
         ],
         compiler_params=pltpu.CompilerParams(vmem_limit_bytes=56 * 2**20, collective_id=2, has_side_effects=True),
         name="reduce",
-    )(state, shard, right, *pieces)
+    )(states, relations, right, *pieces)
 
 
 def finish_kernel(
@@ -829,7 +841,7 @@
 
 
 def finish(width, left, back, ent, ent_state, news, count):
-    steps = 8
+    steps = 4
     full = lambda a: pl.BlockSpec(a.shape, lambda s: (0, 0))
     rows = ent.shape[1]
     return pl.pallas_call(
@@ -867,14 +879,9 @@
     nidx = (neg_owner[0, :, 0] * rows + neg_off[0]).reshape(spans, NEG)
     nidx = jnp.pad(nidx, ((0, 0), (0, SPAN - NEG)), constant_values=rows * BLOCKS).reshape(edges)
     rid = rel_ids[0]
-    at = here()
-    mine = (at["core"] * SHARDS + index_of(at, ("z", "y", "x"))) * GROUP
-    rel_shard = jnp.pad(lax.dynamic_slice_in_dim(relations, mine, GROUP, 0), ((0, 0), (0, wide - width)))
-    rel_state_shard = lax.dynamic_slice_in_dim(rel_state, mine, GROUP, 0)[:, None]
-
     slab, rel_rows = fetch(rid, padded, relations.T)
     right, *pieces, left = bucket(counts[0], ridx, nidx, rid, lhs_rows.reshape(spans, 1, SPAN), padded, rel_rows, slab)
-    back, *news = reduce(width, rel_state_shard, rel_shard, right, pieces)
+    back, *news = reduce(width, rel_state[None], relations.T, right, pieces)
     rel_new, states, new_shard, new_state = finish(
         width, left, back, shard.T, ent_state, [n.reshape(-1, LANES) for n in news], relations.shape[0]
     )

time: 216 us -> 208 us (0.963)
  Pallas kernels: 204 us -> 198 us
  local copies, waits for them, and re-layouts: 5.88 us -> 3.31 us
where the time goes in v4:
time: 208 us; the launch traced here: 207 us
  Pallas kernels  198 us (95%)
  other arithmetic  4.23 us (2%)
  local copies, waits for them, and re-layouts  3.31 us (2%)
    pallas_call x1, Pallas kernels, reduce(): pl.pallas_call(functools.partial(reduce_kernel, width), out_shape=(jax.Sh...  73.4 us
    pallas_call x1, Pallas kernels, bucket(): pl.pallas_call(functools.partial(bucket_kernel, spans, 16), grid=(spans +...  67.5 us
    pallas_call x1, Pallas kernels, fetch(): pl.pallas_call(fetch_kernel, out_shape=(jax.ShapeDtypeStruct((rows * CHUN...  48.3 us
    pallas_call x1, Pallas kernels, finish(): pl.pallas_call(functools.partial(finish_kernel, width), grid=(steps,), ou...  9.29 us

profile of v4, /device:TPU:1, one launch (start us, length us, event | category | flops | bytes accessed | tf_op | source)
XLA Modules:
  0.0 207.5 jit_solution(10483766388809391573)
XLA Ops:
  1.3 0.5 broadcast.15
  1.8 1.4 reduce.8
  3.2 0.1 squeeze.19
  3.3 0.7 broadcast_multiply_fusion
  4.0 1.3 add.11.ridx_ref
  5.3 0.8 multiply_reduce_fusion
  6.1 0.1 mul.24
  6.2 0.6 copy.18
  6.8 1.2 copy.17
  8.0 0.8 pad.9.clone.ent_ref
  8.9 48.3 %fetch.1 = (f32[16384,128]{1,0:T(8,128)}, f32[16384,128]{1,0:T(8,128)}) custom-call(s32[4096]{0:T(1024)} %bitcast.29, f32[256,512]{1,0:T(8,128)} %pad.9.clone.ent_ref, f32[400,4096]{1,0:T(8,128)} %bitcast.22), custom_call_target="tpu_custom_call" | custom-call | tf_op jit(solution)/shard_map/fetch/pallas_call | solution.py:478
  57.2 67.5 %bucket.1 = (f32[13312,128]{1,0:T(8,128)}, f32[4096,128]{1,0:T(8,128)}, f32[4096,128]{1,0:T(8,128)}, f32[5120,128]{1,0:T(8,128)}, f32[256,512]{1,0:T(8,128)}) custom-call(s32[1]{0:T(128)} %bitcast.21.cnt_ref, s32[4096]{0:T(1024)} %add.11.ridx_ref, s32[4096]{0:T(1024)} %bitcast.31, s32[4096]{0:T(1024)} %bitcast.30, s32[8,1,512]{2,1,0:T(1,128)} %bitcast.33, ...), custom_call_target="tpu_custom_call" | custom-call | tf_op jit(solution)/shard_map/bucket/pallas_call | solution.py:637
  124.7 73.4 %reduce.9 = (f32[832,128]{1,0:T(8,128)}, f32[2,4,4,4,32,128]{5,4,3,2,1,0:T(8,128)}, f32[2,4,4,4,32,128]{5,4,3,2,1,0:T(8,128)}, f32[2,4,4,4,40,128]{5,4,3,2,1,0:T(8,128)}) custom-call(f32[1,4096]{1,0:T(1,128)} %bitcast.35, f32[400,4096]{1,0:T(8,128)} %bitcast.23, f32[13312,128]{1,0:T(8,128)} %get-tuple-element.22.right_hbm, ...), custom_call_target="tpu_custom_call" | custom-call | tf_op jit(solution)/shard_map/reduce/pallas_call | solution.py:775
  198.0 9.3 %finish.1 = (f32[400,4096]{1,0:T(8,128)}, f32[1,4096]{1,0:T(1,128)}, f32[400,256]{1,0:T(8,128)}, f32[1,256]{1,0:T(1,128)}) custom-call(f32[256,512]{1,0:T(8,128)} %get-tuple-element.21.left_ref, f32[832,128]{1,0:T(8,128)} %get-tuple-element.26.back_ref, f32[400,256]{1,0:T(8,128)} %bitcast.28, f32[1,256]{1,0:T(1,128)} %state_ref.1, f32[4096,128]{1,0:T(8,128)} %bitcast.25, ...), custom_call_target="tpu_custom_call" | custom-call | tf_op jit(solution)/shard_map/finish/pallas_call | solution.py:847
  (2 shorter events, 0.0 us)

commit v5 on v4

--- a/solution.py
+++ b/solution.py
@@ -454,7 +454,7 @@
             def step(b, carry):
                 for u in range(unroll):
                     j = t * segment + b * unroll + u
-                    got[row(j), :] = rel_rows[rid_ref[j]]
+                    got[row(j), :] = rel_rows[rid_ref[0, j]]
                 return carry
 
             lax.fori_loop(0, segment // unroll, step, 0)
@@ -471,7 +471,7 @@
 
 
 def fetch(rid, ent, relations):
-    edges = rid.shape[0]
+    edges = rid.shape[1]
     width, count = relations.shape
     rows = ent.shape[0] * BLOCKS
     anym = pl.BlockSpec(memory_space=pl.ANY)
@@ -512,54 +512,58 @@
     def _():
         load = pltpu.make_async_copy(slab_hbm, slab.at[pl.ds(0, total)], sem.at[0])
         load.start()
-        slab[pl.ds(total, 8), :] = jnp.zeros((8, LANES), F32)
+        nvec[pl.ds(NEG * CHUNKS, (SPAN - NEG) * CHUNKS), :] = jnp.zeros(((SPAN - NEG) * CHUNKS, LANES), F32)
         racc[...] = jnp.zeros_like(racc)
         nacc[...] = jnp.zeros_like(nacc)
         relacc[...] = jnp.zeros_like(relacc)
         left_ref[...] = jnp.zeros_like(left_ref)
         load.wait()
 
-    def scatter(j, base):
-        rel = row(rid_ref[base + j])
-        rgt = row(ridx_ref[base + j])
-        neg = row(nidx_ref[base + j])
+    def scatter(j, negative):
+        edge = (s - 1) * SPAN + j
+        rel = row(rid_ref[0, edge])
+        rgt = row(ridx_ref[0, edge])
         own = row(j)
         relacc[rel, :] = relacc[rel, :] + grel[own, :]
         racc[rgt, :] = racc[rgt, :] + gr[own, :]
-        nacc[neg, :] = nacc[neg, :] + gn[own, :]
-
-    def gather(j, base):
+        if negative:
+            neg = row(nidx_ref[0, (s - 1) * NEG + j])
+            nacc[neg, :] = nacc[neg, :] + gn[own, :]
+
+    def gather(j, negative):
         own = row(j)
-        rvec[own, :] = slab[row(ridx_ref[base + j]), :]
-        nvec[own, :] = slab[row(nidx_ref[base + j]), :]
-
-    behind = (s - 1) * SPAN
-    ahead = s * SPAN
+        rvec[own, :] = slab[row(ridx_ref[0, s * SPAN + j]), :]
+        if negative:
+            nvec[own, :] = slab[row(nidx_ref[0, s * NEG + j]), :]
 
     def rows_loop(*works):
         def step(b, carry):
             for u in range(unroll):
-                for work, base in works:
-                    work(b * unroll + u, base)
+                for work in works:
+                    work(b * unroll + u, True)
             return carry
 
-        lax.fori_loop(0, SPAN // unroll, step, 0)
+        last = NEG // unroll * unroll
+        lax.fori_loop(0, last // unroll, step, 0)
+        for j in range(last, SPAN):
+            for work in works:
+                work(j, j < NEG)
 
     @pl.when(s == 0)
     def _():
-        rows_loop((gather, ahead))
+        rows_loop(gather)
 
     @pl.when((s > 0) & (s < spans))
     def _():
-        rows_loop((gather, ahead), (scatter, behind))
+        rows_loop(gather, scatter)
 
     @pl.when(s == spans)
     def _():
-        rows_loop((scatter, behind))
+        rows_loop(scatter)
 
     @pl.when(s < spans)
     def _():
-        hot = (lax.broadcasted_iota(jnp.int32, (ent_ref.shape[0], SPAN), 0) == lhs_ref[0]).astype(F32).astype(BF16)
+        hot = (lax.broadcasted_iota(jnp.int32, (ent_ref.shape[0], SPAN), 0) == lhs_ref[...]).astype(F32).astype(BF16)
         eh, el = split(ent_ref[...])
         first = ((0,), (0,))
         last = ((1,), (1,))
@@ -614,20 +618,21 @@
                 nacc[span_of(at[2] + GROUP, 8), :] = pack_tail(relacc[pl.ds(src + 3, GROUP, stride=CHUNKS), :])
             return carry
 
-        lax.fori_loop(0, 2 * SHARDS // 4, shards, 0)
-        copies = [
-            pltpu.make_async_copy(nacc.at[pl.ds(b, ref.shape[0])], ref, sem.at[1 + p])
-            for p, (b, ref) in enumerate(zip(begins, (rel0_hbm, rel1_hbm, rel2_hbm)))
-        ]
-        for copy in copies:
-            copy.start()
+        copies = []
+        for half in range(2):
+            lax.fori_loop(half * SHARDS // 4, (half + 1) * SHARDS // 4, shards, 0)
+            for p, ref in enumerate((rel0_hbm, rel1_hbm, rel2_hbm)):
+                size = SHARDS * PIECE_ROWS[p]
+                src = nacc.at[pl.ds(begins[p] + half * size, size)]
+                copies.append(pltpu.make_async_copy(src, ref.at[pl.ds(half * size, size)], sem.at[1 + len(copies)]))
+                copies[-1].start()
         for copy in copies:
             copy.wait()
         out.wait()
 
 
 def bucket(counts, ridx, nidx, rid, lhs, ent, rel_rows, slab):
-    edges = rid.shape[0]
+    edges = rid.shape[1]
     spans = edges // SPAN
     total = slab.shape[0]
     smem = pl.BlockSpec(memory_space=pltpu.SMEM)
@@ -635,7 +640,7 @@
     vm = lambda r: pltpu.VMEM((r, LANES), F32)
     span_rows = SPAN * CHUNKS
     return pl.pallas_call(
-        functools.partial(bucket_kernel, spans, 16),
+        functools.partial(bucket_kernel, spans, 25),
         grid=(spans + 1,),
         out_shape=(
             jax.ShapeDtypeStruct((BLOCKS * 256 // GROUP * PACK, LANES), F32),
@@ -644,16 +649,16 @@
         ),
         in_specs=[
             smem, smem, smem, smem,
-            pl.BlockSpec((1, 1, SPAN), lambda s: (jnp.minimum(s, spans - 1), 0, 0)),
+            pl.BlockSpec((1, SPAN), lambda s: (0, jnp.minimum(s, spans - 1))),
             pl.BlockSpec(ent.shape, lambda s: (0, 0)),
             pl.BlockSpec((span_rows, LANES), lambda s: (jnp.minimum(s, spans - 1), 0)),
             anym,
         ],
         out_specs=(anym, anym, anym, anym, pl.BlockSpec(ent.shape, lambda s: (0, 0))),
         scratch_shapes=[
-            vm(total + 8), vm(total), vm(total + 8), vm(total),
+            vm(total), vm(total), vm(total), vm(total),
             vm(span_rows), vm(span_rows), vm(span_rows), vm(span_rows), vm(span_rows),
-            pltpu.SemaphoreType.DMA((4,)),
+            pltpu.SemaphoreType.DMA((8,)),
         ],
         compiler_params=pltpu.CompilerParams(vmem_limit_bytes=58 * 2**20),
         name="bucket",
@@ -873,14 +878,10 @@
     rows, width = shard.shape
     wide = CHUNKS * LANES
     padded = jnp.pad(shard, ((0, 0), (0, wide - width)))
-    edges = lhs_rows.shape[1]
-    spans = edges // SPAN
-    ridx = rhs_owner[0, :, 0] * rows + rhs_off[0]
-    nidx = (neg_owner[0, :, 0] * rows + neg_off[0]).reshape(spans, NEG)
-    nidx = jnp.pad(nidx, ((0, 0), (0, SPAN - NEG)), constant_values=rows * BLOCKS).reshape(edges)
-    rid = rel_ids[0]
-    slab, rel_rows = fetch(rid, padded, relations.T)
-    right, *pieces, left = bucket(counts[0], ridx, nidx, rid, lhs_rows.reshape(spans, 1, SPAN), padded, rel_rows, slab)
+    ridx = rhs_owner[:, :, 0] * rows + rhs_off
+    nidx = neg_owner[:, :, 0] * rows + neg_off
+    slab, rel_rows = fetch(rel_ids, padded, relations.T)
+    right, *pieces, left = bucket(counts[0], ridx, nidx, rel_ids, lhs_rows, padded, rel_rows, slab)
     back, *news = reduce(width, rel_state[None], relations.T, right, pieces)
     rel_new, states, new_shard, new_state = finish(
         width, left, back, shard.T, ent_state, [n.reshape(-1, LANES) for n in news], relations.shape[0]

time: 208 us -> 204 us (0.981)
  no operation moved by 1% of the time
where the time goes in v5:
time: 204 us; the launch traced here: 203 us
  Pallas kernels  197 us (97%)
  other arithmetic  2.72 us (1%)
    pallas_call x1, Pallas kernels, reduce(): pl.pallas_call(functools.partial(reduce_kernel, width), out_shape=(jax.Sh...  73.4 us
    pallas_call x1, Pallas kernels, bucket(): pl.pallas_call(functools.partial(bucket_kernel, spans, 25), grid=(spans +...  66 us
    pallas_call x1, Pallas kernels, fetch(): pl.pallas_call(fetch_kernel, out_shape=(jax.ShapeDtypeStruct((rows * CHUN...  48.3 us
    pallas_call x1, Pallas kernels, finish(): pl.pallas_call(functools.partial(finish_kernel, width), grid=(steps,), ou...  9.29 us

profile of v5, /device:TPU:1, one launch (start us, length us, event | category | flops | bytes accessed | tf_op | source)
XLA Modules:
  0.0 203.1 jit_solution(17871019386570382514)
XLA Ops:
  1.3 1.4 bitcast_add_fusion.1.ridx_ref
  2.6 1.4 bitcast_add_fusion.nidx_ref
  4.0 1.2 copy.17
  5.2 0.8 pad.4.clone.ent_ref
  6.0 48.3 %fetch.1 = (f32[16384,128]{1,0:T(8,128)}, f32[16384,128]{1,0:T(8,128)}) custom-call(s32[1,4096]{1,0:T(1,128)} %rid_ref.3, f32[256,512]{1,0:T(8,128)} %pad.4.clone.ent_ref, f32[400,4096]{1,0:T(8,128)} %bitcast.19), custom_call_target="tpu_custom_call" | custom-call | tf_op jit(solution)/shard_map/fetch/pallas_call | solution.py:478
  54.3 66.0 %bucket.1 = (f32[13312,128]{1,0:T(8,128)}, f32[4096,128]{1,0:T(8,128)}, f32[4096,128]{1,0:T(8,128)}, f32[5120,128]{1,0:T(8,128)}, f32[256,512]{1,0:T(8,128)}) custom-call(s32[1]{0:T(128)} %bitcast.18.cnt_ref, s32[1,4096]{1,0:T(1,128)} %bitcast_add_fusion.1.ridx_ref, s32[1,4000]{1,0:T(1,128)} %bitcast_add_fusion.nidx_ref, s32[1,4096]{1,0:T(1,128)} %rid_ref.3, ...), custom_call_target="tpu_custom_call" | custom-call | tf_op jit(solution)/shard_map/bucket/pallas_call | solution.py:642
  120.3 73.4 %reduce.1 = (f32[832,128]{1,0:T(8,128)}, f32[2,4,4,4,32,128]{5,4,3,2,1,0:T(8,128)}, f32[2,4,4,4,32,128]{5,4,3,2,1,0:T(8,128)}, f32[2,4,4,4,40,128]{5,4,3,2,1,0:T(8,128)}) custom-call(f32[1,4096]{1,0:T(1,128)} %bitcast.26, f32[400,4096]{1,0:T(8,128)} %bitcast.20, f32[13312,128]{1,0:T(8,128)} %get-tuple-element.22.right_hbm, ...), custom_call_target="tpu_custom_call" | custom-call | tf_op jit(solution)/shard_map/reduce/pallas_call | solution.py:780
  193.6 9.3 %finish.1 = (f32[400,4096]{1,0:T(8,128)}, f32[1,4096]{1,0:T(1,128)}, f32[400,256]{1,0:T(8,128)}, f32[1,256]{1,0:T(1,128)}) custom-call(f32[256,512]{1,0:T(8,128)} %get-tuple-element.21.left_ref, f32[832,128]{1,0:T(8,128)} %get-tuple-element.26.back_ref, f32[400,256]{1,0:T(8,128)} %bitcast.25, f32[1,256]{1,0:T(1,128)} %state_ref.1, f32[4096,128]{1,0:T(8,128)} %bitcast.22, ...), custom_call_target="tpu_custom_call" | custom-call | tf_op jit(solution)/shard_map/finish/pallas_call | solution.py:852

commit v6 on v5

--- a/solution.py
+++ b/solution.py
@@ -588,8 +588,10 @@
 
     @pl.when(s == spans)
     def _():
-        def right_member(m, carry):
-            for part in range(len(PART_SUM)):
+        middle = len(PART_SUM) // 2
+
+        def right_member(m, carry, parts):
+            for part in parts:
                 for k in range(256 // GROUP // len(PART_SUM)):
                     at = part * (256 // GROUP // len(PART_SUM)) + k
                     src = pl.multiple_of((m * 256 + at * GROUP) * CHUNKS, 128)
@@ -603,9 +605,12 @@
                     slab[span_of(out + 96, 8), :] = pack_tail(planes[3])
             return carry
 
-        lax.fori_loop(0, BLOCKS, right_member, 0)
-        out = pltpu.make_async_copy(slab.at[pl.ds(0, right_hbm.shape[0])], right_hbm, sem.at[0])
-        out.start()
+        outs = []
+        for k, parts in enumerate((range(middle), range(middle, 2 * middle))):
+            lax.fori_loop(0, BLOCKS, functools.partial(right_member, parts=parts), 0)
+            stretch = pl.ds(k * right_hbm.shape[0] // 2, right_hbm.shape[0] // 2)
+            outs.append(pltpu.make_async_copy(slab.at[stretch], right_hbm.at[stretch], sem.at[7 * k]))
+            outs[-1].start()
         begins = (0, 2 * SHARDS * PIECE_ROWS[0], 2 * SHARDS * (PIECE_ROWS[0] + PIECE_ROWS[1]))
 
         def shards(i, carry):
@@ -628,7 +633,8 @@
                 copies[-1].start()
         for copy in copies:
             copy.wait()
-        out.wait()
+        for out in outs:
+            out.wait()
 
 
 def bucket(counts, ridx, nidx, rid, lhs, ent, rel_rows, slab):

time: 204 us -> 205 us (level)
  no operation moved by 1% of the time
where the time goes in v6:
time: 205 us; the launch traced here: 204 us
  Pallas kernels  198 us (97%)
  other arithmetic  2.72 us (1%)
    pallas_call x1, Pallas kernels, reduce(): pl.pallas_call(functools.partial(reduce_kernel, width), out_shape=(jax.Sh...  73.4 us
    pallas_call x1, Pallas kernels, bucket(): pl.pallas_call(functools.partial(bucket_kernel, spans, 25), grid=(spans +...  67.1 us
    pallas_call x1, Pallas kernels, fetch(): pl.pallas_call(fetch_kernel, out_shape=(jax.ShapeDtypeStruct((rows * CHUN...  48.3 us
    pallas_call x1, Pallas kernels, finish(): pl.pallas_call(functools.partial(finish_kernel, width), grid=(steps,), ou...  9.29 us

profile of v6, /device:TPU:1, one launch (start us, length us, event | category | flops | bytes accessed | tf_op | source)
XLA Modules:
  0.0 204.3 jit_solution(7889356664385752698)
XLA Ops:
  1.3 1.4 bitcast_add_fusion.1.ridx_ref
  2.6 1.4 bitcast_add_fusion.nidx_ref
  4.0 1.2 copy.17
  5.2 0.8 pad.4.clone.ent_ref
  6.0 48.3 %fetch.1 = (f32[16384,128]{1,0:T(8,128)}, f32[16384,128]{1,0:T(8,128)}) custom-call(s32[1,4096]{1,0:T(1,128)} %rid_ref.3, f32[256,512]{1,0:T(8,128)} %pad.4.clone.ent_ref, f32[400,4096]{1,0:T(8,128)} %bitcast.19), custom_call_target="tpu_custom_call" | custom-call | tf_op jit(solution)/shard_map/fetch/pallas_call | solution.py:478
  54.3 67.1 %bucket.1 = (f32[13312,128]{1,0:T(8,128)}, f32[4096,128]{1,0:T(8,128)}, f32[4096,128]{1,0:T(8,128)}, f32[5120,128]{1,0:T(8,128)}, f32[256,512]{1,0:T(8,128)}) custom-call(s32[1]{0:T(128)} %bitcast.18.cnt_ref, s32[1,4096]{1,0:T(1,128)} %bitcast_add_fusion.1.ridx_ref, s32[1,4000]{1,0:T(1,128)} %bitcast_add_fusion.nidx_ref, s32[1,4096]{1,0:T(1,128)} %rid_ref.3, ...), custom_call_target="tpu_custom_call" | custom-call | tf_op jit(solution)/shard_map/bucket/pallas_call | solution.py:648
  121.4 73.4 %reduce.1 = (f32[832,128]{1,0:T(8,128)}, f32[2,4,4,4,32,128]{5,4,3,2,1,0:T(8,128)}, f32[2,4,4,4,32,128]{5,4,3,2,1,0:T(8,128)}, f32[2,4,4,4,40,128]{5,4,3,2,1,0:T(8,128)}) custom-call(f32[1,4096]{1,0:T(1,128)} %bitcast.26, f32[400,4096]{1,0:T(8,128)} %bitcast.20, f32[13312,128]{1,0:T(8,128)} %get-tuple-element.22.right_hbm, ...), custom_call_target="tpu_custom_call" | custom-call | tf_op jit(solution)/shard_map/reduce/pallas_call | solution.py:786
  194.8 9.3 %finish.1 = (f32[400,4096]{1,0:T(8,128)}, f32[1,4096]{1,0:T(1,128)}, f32[400,256]{1,0:T(8,128)}, f32[1,256]{1,0:T(1,128)}) custom-call(f32[256,512]{1,0:T(8,128)} %get-tuple-element.21.left_ref, f32[832,128]{1,0:T(8,128)} %get-tuple-element.26.back_ref, f32[400,256]{1,0:T(8,128)} %bitcast.25, f32[1,256]{1,0:T(1,128)} %state_ref.1, f32[4096,128]{1,0:T(8,128)} %bitcast.22, ...), custom_call_target="tpu_custom_call" | custom-call | tf_op jit(solution)/shard_map/finish/pallas_call | solution.py:858

commit v7 on v5

--- a/solution.py
+++ b/solution.py
@@ -640,7 +640,7 @@
     vm = lambda r: pltpu.VMEM((r, LANES), F32)
     span_rows = SPAN * CHUNKS
     return pl.pallas_call(
-        functools.partial(bucket_kernel, spans, 25),
+        functools.partial(bucket_kernel, spans, 50),
         grid=(spans + 1,),
         out_shape=(
             jax.ShapeDtypeStruct((BLOCKS * 256 // GROUP * PACK, LANES), F32),

time: 204 us -> 203 us (level)
  no operation moved by 1% of the time
where the time goes in v7:
time: 203 us
  Pallas kernels  196 us (97%)
  other arithmetic  2.72 us (1%)
    pallas_call x1, Pallas kernels, reduce(): pl.pallas_call(functools.partial(reduce_kernel, width), out_shape=(jax.Sh...  73.4 us
    pallas_call x1, Pallas kernels, bucket(): pl.pallas_call(functools.partial(bucket_kernel, spans, 50), grid=(spans +...  65.4 us
    pallas_call x1, Pallas kernels, fetch(): pl.pallas_call(fetch_kernel, out_shape=(jax.ShapeDtypeStruct((rows * CHUN...  48.3 us
    pallas_call x1, Pallas kernels, finish(): pl.pallas_call(functools.partial(finish_kernel, width), grid=(steps,), ou...  9.29 us

profile of v7, /device:TPU:1, one launch (start us, length us, event | category | flops | bytes accessed | tf_op | source)
XLA Modules:
  0.0 202.5 jit_solution(14858035032035339807)
XLA Ops:
  1.3 1.4 bitcast_add_fusion.1.ridx_ref
  2.6 1.4 bitcast_add_fusion.nidx_ref
  4.0 1.2 copy.17
  5.2 0.8 pad.4.clone.ent_ref
  6.0 48.3 %fetch.1 = (f32[16384,128]{1,0:T(8,128)}, f32[16384,128]{1,0:T(8,128)}) custom-call(s32[1,4096]{1,0:T(1,128)} %rid_ref.3, f32[256,512]{1,0:T(8,128)} %pad.4.clone.ent_ref, f32[400,4096]{1,0:T(8,128)} %bitcast.19), custom_call_target="tpu_custom_call" | custom-call | tf_op jit(solution)/shard_map/fetch/pallas_call | solution.py:478
  54.3 65.4 %bucket.1 = (f32[13312,128]{1,0:T(8,128)}, f32[4096,128]{1,0:T(8,128)}, f32[4096,128]{1,0:T(8,128)}, f32[5120,128]{1,0:T(8,128)}, f32[256,512]{1,0:T(8,128)}) custom-call(s32[1]{0:T(128)} %bitcast.18.cnt_ref, s32[1,4096]{1,0:T(1,128)} %bitcast_add_fusion.1.ridx_ref, s32[1,4000]{1,0:T(1,128)} %bitcast_add_fusion.nidx_ref, s32[1,4096]{1,0:T(1,128)} %rid_ref.3, ...), custom_call_target="tpu_custom_call" | custom-call | tf_op jit(solution)/shard_map/bucket/pallas_call | solution.py:642
  119.7 73.4 %reduce.1 = (f32[832,128]{1,0:T(8,128)}, f32[2,4,4,4,32,128]{5,4,3,2,1,0:T(8,128)}, f32[2,4,4,4,32,128]{5,4,3,2,1,0:T(8,128)}, f32[2,4,4,4,40,128]{5,4,3,2,1,0:T(8,128)}) custom-call(f32[1,4096]{1,0:T(1,128)} %bitcast.26, f32[400,4096]{1,0:T(8,128)} %bitcast.20, f32[13312,128]{1,0:T(8,128)} %get-tuple-element.22.right_hbm, ...), custom_call_target="tpu_custom_call" | custom-call | tf_op jit(solution)/shard_map/reduce/pallas_call | solution.py:780
  193.1 9.3 %finish.1 = (f32[400,4096]{1,0:T(8,128)}, f32[1,4096]{1,0:T(1,128)}, f32[400,256]{1,0:T(8,128)}, f32[1,256]{1,0:T(1,128)}) custom-call(f32[256,512]{1,0:T(8,128)} %get-tuple-element.21.left_ref, f32[832,128]{1,0:T(8,128)} %get-tuple-element.26.back_ref, f32[400,256]{1,0:T(8,128)} %bitcast.25, f32[1,256]{1,0:T(1,128)} %state_ref.1, f32[4096,128]{1,0:T(8,128)} %bitcast.22, ...), custom_call_target="tpu_custom_call" | custom-call | tf_op jit(solution)/shard_map/finish/pallas_call | solution.py:852
